TPU v7x, 32 devices: a whole 2x2x4 slice. The times are simulated.
32 devices in a mesh: section: 4 (over y, core), expert: 8 (over z, x).
Axes of the slice: x: 2, y: 2, z: 4, core: 2. Of those that a mesh axis runs over, the one named last changes fastest.
Arguments:
- acts_fwd: bfloat16 [4, 1024, 7168], P('section', 'expert'), may hold values from -6 to 6
- routes_fwd: int32 [4, 1024, 1], P('section', 'expert'), may hold values from 0 to 1; in each aligned block of 128 rows (0 to 127, 128 to 255, ..., all dimensions but the last counted through in order) at most 72 rows name the same one
- gates_fwd: float32 [4, 1024, 1], P('section', 'expert'), may hold values from 0.2 to 1.5
- stash_bwd: bfloat16 [4, 1024, 7168], P('section', 'expert'), may hold values from -6 to 6
- grads_bwd: bfloat16 [4, 1024, 7168], P('section', 'expert'), may hold values from -6 to 6
- routes_bwd: int32 [4, 1024, 1], P('section', 'expert'), may hold values from 0 to 1; in each aligned block of 128 rows (0 to 127, 128 to 255, ..., all dimensions but the last counted through in order) at most 72 rows name the same one
- gates_bwd: float32 [4, 1024, 1], P('section', 'expert'), may hold values from 0.2 to 1.5
- gain: float32 [4, 7168], P('section'), may hold values from 0.1 to 1.9
- w_gate: bfloat16 [4, 7168, 2048], P('section', None, 'expert'), may hold values from -0.0625 to 0.0625
- w_up: bfloat16 [4, 7168, 2048], P('section', None, 'expert'), may hold values from -0.0625 to 0.0625
- w_down: bfloat16 [4, 2048, 7168], P('section', 'expert'), may hold values from -0.1875 to 0.1875
Outputs:
- fwd_next: bfloat16 [4, 1024, 7168], P('section', 'expert')
- grad_next: bfloat16 [4, 1024, 7168], P('section', 'expert')
Inputs may be any that keep to these rules, and one draw needn't show every extreme that they name: `routes_fwd`: each row names 1 different experts. In the rows of one device (aligned blocks of 128 rows of one layer) no expert is named by more than 72 rows, a bound that some block reaches. `routes_bwd`: each row names 1 different experts. In the rows of one device (aligned blocks of 128 rows of one layer) no expert is named by more than 72 rows, a bound that some block reaches.
All inputs are finite; a program needn't handle non-finite values.
Results may differ from a plain program's by a relative error of at most 0.006.
Values may be sent and summed in bfloat16 or wider, within the bound.
A program may use at most 128 MiB of HBM per device.

v0:
```python
import jax
import jax.numpy as jnp
from jax import lax
from jax.sharding import PartitionSpec as P

SHARDS = 4
TOP = 1


EPS = 1e-06


def from_behind(value, axis, by):
    devices = lax.axis_size(axis)
    return lax.ppermute(value, axis, [(i, (i + by) % devices) for i in range(devices)])


def normed(token_rows, gain_row):
    values = token_rows.astype(jnp.float32)
    factor = lax.rsqrt(jnp.mean(values * values, axis=-1, keepdims=True) + EPS)
    return values * factor * gain_row


def slot_tables(route_ids, gate_vals, experts_n, capacity):
    tok_rows, top_n = route_ids.shape
    flat_ids = route_ids.reshape(-1)
    one_hot = (flat_ids[:, None] == jnp.arange(experts_n, dtype=jnp.int32)[None, :]).astype(
        jnp.int32
    )
    slot_ids = jnp.sum((jnp.cumsum(one_hot, axis=0) - one_hot) * one_hot, axis=1)
    position = flat_ids * capacity + slot_ids
    places = jnp.arange(experts_n * capacity, dtype=jnp.int32)
    hit = position[None, :] == places[:, None]
    pair_token = jnp.arange(tok_rows * top_n, dtype=jnp.int32) // top_n
    owner = jnp.sum(jnp.where(hit, pair_token[None, :], 0), axis=1)
    filled = jnp.any(hit, axis=1)
    slot_gate = jnp.sum(jnp.where(hit, gate_vals.reshape(-1)[None, :], jnp.float32(0.0)), axis=1)
    return (position.reshape(tok_rows, top_n), owner, filled, slot_gate)


def pack_rows(owner, filled, token_rows, experts_n, capacity):
    picked = jnp.take(token_rows, owner, axis=0)
    packed = jnp.where(filled[:, None], picked, jnp.zeros_like(picked))
    return packed.reshape(experts_n, capacity, token_rows.shape[1])


def pack_scaled(owner, slot_gate, token_rows, experts_n, capacity):
    picked = jnp.take(token_rows, owner, axis=0).astype(jnp.float32) * slot_gate[:, None]
    return picked.astype(jnp.bfloat16).reshape(experts_n, capacity, token_rows.shape[1])


def spread(buffer, copies):
    experts_n, slots, features = buffer.shape
    return jnp.broadcast_to(buffer[:, None], (experts_n, copies, slots, features)).reshape(
        experts_n * copies, slots, features
    )


def expert_forward(token_rows, gate_cols, up_cols, down_rows):
    pre_gate = jnp.dot(token_rows, gate_cols, preferred_element_type=jnp.float32)
    pre_up = jnp.dot(token_rows, up_cols, preferred_element_type=jnp.float32)
    hidden = (pre_gate * jax.nn.sigmoid(pre_gate) * pre_up).astype(jnp.bfloat16)
    return jnp.dot(hidden, down_rows, preferred_element_type=jnp.float32)


def expert_backward(token_rows, upstream, gate_cols, up_cols, down_rows):
    pre_gate = jnp.dot(token_rows, gate_cols, preferred_element_type=jnp.float32)
    pre_up = jnp.dot(token_rows, up_cols, preferred_element_type=jnp.float32)
    contract = (((1,), (1,)), ((), ()))
    grad_hidden = lax.dot_general(upstream, down_rows, contract, preferred_element_type=jnp.float32)
    sigmoid_gate = jax.nn.sigmoid(pre_gate)
    grad_gate = (
        grad_hidden * pre_up * sigmoid_gate * (1.0 + pre_gate * (1.0 - sigmoid_gate))
    ).astype(jnp.bfloat16)
    grad_up = (grad_hidden * pre_gate * sigmoid_gate).astype(jnp.bfloat16)
    first = lax.dot_general(grad_gate, gate_cols, contract, preferred_element_type=jnp.float32)
    second = lax.dot_general(grad_up, up_cols, contract, preferred_element_type=jnp.float32)
    return first + second


def unfold_shards(returned, experts_n):
    sources, slots, features = returned.shape
    grouped = returned.reshape(experts_n, SHARDS, slots, features).astype(jnp.float32)
    return jnp.sum(grouped, axis=1).reshape(experts_n * slots, features)


def local(
    acts_fwd,
    routes_fwd,
    gates_fwd,
    stash_bwd,
    grads_bwd,
    routes_bwd,
    gates_bwd,
    gain,
    w_gate,
    w_up,
    w_down,
):
    devices = lax.axis_size("expert")
    experts_n = devices // SHARDS
    tok_rows = acts_fwd.shape[1]
    capacity = min(tok_rows, 9 * tok_rows * TOP // (8 * experts_n))
    gate_cols = w_gate[0]
    up_cols = w_up[0]
    down_rows = w_down[0]
    gain_row = gain[0]
    entering = acts_fwd[0]
    place_fwd, owner_fwd, filled_fwd, unused_gate = slot_tables(
        routes_fwd[0], gates_fwd[0], experts_n, capacity
    )
    send_fwd = spread(
        pack_rows(
            owner_fwd,
            filled_fwd,
            normed(entering, gain_row).astype(jnp.bfloat16),
            experts_n,
            capacity,
        ),
        SHARDS,
    )
    stashed = stash_bwd[0]
    upstream = grads_bwd[0]
    place_bwd, owner_bwd, filled_bwd, slot_gate = slot_tables(
        routes_bwd[0], gates_bwd[0], experts_n, capacity
    )
    send_rows = spread(
        pack_rows(
            owner_bwd,
            filled_bwd,
            normed(stashed, gain_row).astype(jnp.bfloat16),
            experts_n,
            capacity,
        ),
        SHARDS,
    )
    send_grads = spread(pack_scaled(owner_bwd, slot_gate, upstream, experts_n, capacity), SHARDS)
    received = lax.all_to_all(send_fwd, "expert", split_axis=0, concat_axis=0, tiled=True)
    sources, slots, features = received.shape
    flat_rows = received.reshape(sources * slots, features)
    result = expert_forward(flat_rows, gate_cols, up_cols, down_rows)
    back_fwd = lax.all_to_all(
        result.astype(jnp.bfloat16).reshape(sources, slots, features),
        "expert",
        split_axis=0,
        concat_axis=0,
        tiled=True,
    )
    received = (
        lax.all_to_all(send_rows, "expert", split_axis=0, concat_axis=0, tiled=True),
        lax.all_to_all(send_grads, "expert", split_axis=0, concat_axis=0, tiled=True),
    )
    received_rows = received[0]
    sources, slots, features = received_rows.shape
    flat_rows = received_rows.reshape(sources * slots, features)
    flat_grads = received[1].reshape(sources * slots, features)
    result = expert_backward(flat_rows, flat_grads, gate_cols, up_cols, down_rows)
    back_bwd = lax.all_to_all(
        result.astype(jnp.bfloat16).reshape(sources, slots, features),
        "expert",
        split_axis=0,
        concat_axis=0,
        tiled=True,
    )
    summed_fwd = unfold_shards(back_fwd, experts_n)
    picked_fwd = jnp.take(summed_fwd, place_fwd, axis=0)
    mixture = jnp.sum(gates_fwd[0][:, :, None] * picked_fwd, axis=1)
    layer_out = (entering.astype(jnp.float32) + mixture).astype(jnp.bfloat16)
    summed_bwd = unfold_shards(back_bwd, experts_n)
    grad_normed = jnp.sum(jnp.take(summed_bwd, place_bwd, axis=0), axis=1)

    def norm_only(values):
        return normed(values, gain_row)

    unused, pullback = jax.vjp(norm_only, stashed.astype(jnp.float32))
    grad_input = (upstream.astype(jnp.float32) + pullback(grad_normed)[0]).astype(jnp.bfloat16)
    fwd_next = from_behind(layer_out[None], "section", 1)
    grad_next = from_behind(grad_input[None], "section", -1)
    return (fwd_next, grad_next)


def solution(mesh):
    return jax.shard_map(
        local,
        mesh=mesh,
        in_specs=(
            P("section", "expert", None),
            P("section", "expert", None),
            P("section", "expert", None),
            P("section", "expert", None),
            P("section", "expert", None),
            P("section", "expert", None),
            P("section", "expert", None),
            P("section", None),
            P("section", None, "expert"),
            P("section", None, "expert"),
            P("section", "expert", None),
        ),
        out_specs=(P("section", "expert", None), P("section", "expert", None)),
        check_vma=False,
    )
```

profile of v0, /device:TPU:0, one launch (start us, length us, event | category | flops | bytes accessed | tf_op | source)
XLA Modules:
  0.0 1083.4 jit_solution(9331914232818609912)
XLA Ops:
  0.6 0.7 fusion.66
  1.4 0.2 reduce_window_sum.18
  1.5 0.8 select_reduce_fusion.3
  2.4 0.7 multiply_add_fusion.1
  3.0 0.1 select_reduce_fusion.1
  3.2 0.1 fusion.64
  3.3 1.9 fusion.9
  5.3 2.0 fusion.11
  7.3 3.2 gather_fusion.3
  10.5 1.9 select_select_fusion
  12.4 4.2 broadcast_in_dim.116
  16.6 0.0 copy-start
  16.6 7.4 all-to-all-start.3
  24.0 0.0 copy-done
  24.0 0.0 copy-start.8
  24.0 3.2 gather_fusion.2
  27.3 0.0 copy-done.8
  27.3 0.1 select_reduce_fusion
  27.4 3.6 multiply_convert_fusion
  30.9 173.4 %all-to-all-done.3 = bf16[8,72,7168]{2,1,0:T(8,128)(2,1)} async-done(((bf16[8,72,7168]{2,1,0:T(8,128)(2,1)}), bf16[8,72,7168]{2,1,0:T(8,128)(2,1)}, u32[]{:S(2)}, u32[]{:S(2)}) %all-to-all-start.3) | async-done | bytes 8257568 | tf_op jit(solution)/shard_map/all_to_all | solution.py:150
  204.3 5.8 broadcast_in_dim.113
  210.2 5.2 all-to-all-start.2
  215.3 6.7 fusion.27
  222.0 172.5 %all-to-all-done.2 = bf16[8,72,7168]{2,1,0:T(8,128)(2,1)} async-done(((bf16[8,72,7168]{2,1,0:T(8,128)(2,1)}), bf16[8,72,7168]{2,1,0:T(8,128)(2,1)}, u32[]{:S(2)}, u32[]{:S(2)}) %all-to-all-start.2) | async-done | bytes 8257568 | tf_op jit(solution)/shard_map/all_to_all | solution.py:151
  394.5 6.7 fusion.17
  401.3 19.8 %fusion.25 = f32[576,7168]{1,0:T(8,128)} fusion(bf16[1,7168,256]{2,1,0:T(8,128)(2,1)} %param.23, f32[576,256]{1,0:T(8,128)S(1)} %fusion.17, bf16[576,7168]{1,0:T(8,128)(2,1)} %bitcast.31, bf16[1,7168,256]{2,1,0:T(8,128)(2,1)} %param.24, f32[576,256]{1,0:T(8,128)S(1)} %fusion.27), kind=kOutput, calls=%fused_computation.44 | convolution fusion | flops 4229332992 | bytes 33292288 | tf_op jit(solution)/shard_map/dot_general | solution.py:76
  421.1 12.6 %add_convert_fusion = bf16[576,7168]{1,0:T(8,128)(2,1)} fusion(f32[576,7168]{1,0:T(8,128)} %fusion.25, bf16[1,7168,256]{2,1,0:T(8,128)(2,1)} %param.24, f32[576,256]{1,0:T(8,128)S(1)} %fusion.17, f32[576,256]{1,0:T(8,128)S(1)} %fusion.27), kind=kOutput, calls=%fused_computation.7 | convolution fusion | flops 2123071488 | bytes 29622272 | tf_op jit(solution)/shard_map/dot_general | solution.py:77
  433.7 5.1 all-to-all-start.4
  438.8 0.0 copy-done.6
  438.8 0.1 fusion.67
  438.9 0.2 reduce_window_sum.17
  439.1 0.0 copy-done.5
  439.1 0.2 select_reduce_fusion.4
  439.3 0.1 select_reduce_fusion.2
  439.4 0.1 fusion.65
  439.5 1.9 fusion.5
  441.5 176.5 %all-to-all-done.4 = bf16[8,72,7168]{2,1,0:T(8,128)(2,1)} async-done(((bf16[8,72,7168]{2,1,0:T(8,128)(2,1)}), bf16[8,72,7168]{2,1,0:T(8,128)(2,1)}, u32[]{:S(2)}, u32[]{:S(2)}) %all-to-all-start.4) | async-done | bytes 8257568 | tf_op jit(solution)/shard_map/all_to_all | solution.py:158
  618.0 7.2 convert_reduce_fusion
  625.2 7.2 gather_fusion.4
  632.4 0.0 copy-done.4
  632.4 5.5 fusion.12
  637.9 6.8 gather_fusion
  644.7 1.9 select_select_fusion.1
  646.6 1.0 broadcast_in_dim.107
  647.6 0.0 copy-start.3
  647.6 184.9 %all_to_all.25 = bf16[8,72,7168]{2,1,0:T(8,128)(2,1)S(1)} all-to-all(bf16[8,72,7168]{2,1,0:T(8,128)(2,1)S(1)} %bitcast.150), channel_id=1, replica_groups=mesh['section'=4,'expert'=8] {'expert'}, dimensions={0} | all-to-all | bytes 16515072 | tf_op jit(solution)/shard_map/all_to_all | solution.py:138
  832.5 3.2 copy-done.1
  835.7 0.0 copy-done.3
  835.7 2.3 fusion.29
  838.0 17.4 %convolution_convert_fusion = bf16[576,7168]{1,0:T(8,128)(2,1)} fusion(bf16[1,256,7168]{2,1,0:T(8,128)(2,1)} %param.25, bf16[576,7168]{1,0:T(8,128)(2,1)} %bitcast.147, bf16[1,7168,256]{2,1,0:T(8,128)(2,1)} %param.24, f32[576,256]{1,0:T(8,128)S(1)} %fusion.29), kind=kOutput, calls=%fused_computation.8 | convolution fusion | flops 4232871936 | bytes 24444928 | tf_op jit(solution)/shard_map/dot_general | solution.py:63
  855.3 5.0 all-to-all-start.1
  860.3 5.1 fusion.14
  865.4 0.2 collective-permute-start.1
  865.6 173.6 %all-to-all-done.1 = bf16[8,72,7168]{2,1,0:T(8,128)(2,1)} async-done(((bf16[8,72,7168]{2,1,0:T(8,128)(2,1)}), bf16[8,72,7168]{2,1,0:T(8,128)(2,1)}, u32[]{:S(2)}, u32[]{:S(2)}) %all-to-all-start.1) | async-done | bytes 8257568 | tf_op jit(solution)/shard_map/all_to_all | solution.py:142
  1039.2 7.2 convert_reduce_fusion.1
  1046.4 7.3 gather_fusion.1
  1053.7 0.0 copy-done.2
  1053.7 0.0 copy-done.7
  1053.7 2.7 fusion.8
  1056.4 0.1 collective-permute-start
  1056.5 0.0 collective-permute-done.1
  1056.5 22.6 %collective-permute-done = bf16[1,128,7168]{2,1,0:T(8,128)(2,1)S(1)} collective-permute-done((bf16[1,128,7168]{2,1,0:T(8,128)(2,1)S(1)}, bf16[1,128,7168]{2,1,0:T(8,128)(2,1)S(1)}, u32[]{:S(2)}, u32[]{:S(2)}) %collective-permute-start) | collective-permute-done | bytes 1835040 | tf_op jit(solution)/shard_map/ppermute | solution.py:15
  1079.1 1.2 copy.15
  1080.4 2.8 copy.16
  (20 shorter events, 0.1 us)
Async XLA Ops:
  16.6 7.4 copy-start
  16.6 187.7 %all-to-all-start.3 = ((bf16[8,72,7168]{2,1,0:T(8,128)(2,1)}), bf16[8,72,7168]{2,1,0:T(8,128)(2,1)}, u32[]{:S(2)}, u32[]{:S(2)}) async-start(bf16[8,72,7168]{2,1,0:T(8,128)(2,1)} %bitcast.148), calls=%async_computation.3 | async-start | bytes 16515072 | tf_op jit(solution)/shard_map/all_to_all | solution.py:150
  24.0 3.3 copy-start.8
  210.2 184.4 %all-to-all-start.2 = ((bf16[8,72,7168]{2,1,0:T(8,128)(2,1)}), bf16[8,72,7168]{2,1,0:T(8,128)(2,1)}, u32[]{:S(2)}, u32[]{:S(2)}) async-start(bf16[8,72,7168]{2,1,0:T(8,128)(2,1)} %bitcast.149), calls=%async_computation.2 | async-start | bytes 16515072 | tf_op jit(solution)/shard_map/all_to_all | solution.py:151
  433.7 5.1 copy-start.6
  433.7 5.4 copy-start.5
  433.7 184.3 %all-to-all-start.4 = ((bf16[8,72,7168]{2,1,0:T(8,128)(2,1)}), bf16[8,72,7168]{2,1,0:T(8,128)(2,1)}, u32[]{:S(2)}, u32[]{:S(2)}) async-start(bf16[8,72,7168]{2,1,0:T(8,128)(2,1)} %bitcast.144), calls=%async_computation.4 | async-start | bytes 16515072 | tf_op jit(solution)/shard_map/all_to_all | solution.py:158
  625.2 7.2 copy-start.4
  647.6 188.0 %copy-start.3 = (bf16[1,7168,256]{2,1,0:T(8,128)(2,1)S(1)}, bf16[1,7168,256]{2,1,0:T(8,128)(2,1)}, u32[]{:S(2)}) copy-start(bf16[1,7168,256]{2,1,0:T(8,128)(2,1)} %param.23) | copy-start | bytes 11010052
  832.5 3.2 copy-start.1
  855.3 183.9 %all-to-all-start.1 = ((bf16[8,72,7168]{2,1,0:T(8,128)(2,1)}), bf16[8,72,7168]{2,1,0:T(8,128)(2,1)}, u32[]{:S(2)}, u32[]{:S(2)}) async-start(bf16[8,72,7168]{2,1,0:T(8,128)(2,1)} %bitcast.145), calls=%async_computation.1 | async-start | bytes 16515072 | tf_op jit(solution)/shard_map/all_to_all | solution.py:142
  865.4 191.1 %collective-permute-start.1 = (bf16[1,128,7168]{2,1,0:T(8,128)(2,1)}, bf16[1,128,7168]{2,1,0:T(8,128)(2,1)}, u32[]{:S(2)}, u32[]{:S(2)}) collective-permute-start(bf16[1,128,7168]{2,1,0:T(8,128)(2,1)} %fusion.14), channel_id=1, source_target_pairs={{0,24},{8,0},{16,8},{24,16},{1,25},{9,1},{17,9},{25,17},{2,26},{10... | collective-permute-start | bytes 5505032 | tf_op jit(solution)/shard_map/ppermute | solution.py:15
  1046.4 7.3 copy-start.2
  1046.4 7.3 copy-start.7
  1056.4 22.7 %collective-permute-start = (bf16[1,128,7168]{2,1,0:T(8,128)(2,1)S(1)}, bf16[1,128,7168]{2,1,0:T(8,128)(2,1)S(1)}, u32[]{:S(2)}, u32[]{:S(2)}) collective-permute-start(bf16[1,128,7168]{2,1,0:T(8,128)(2,1)S(1)} %fusion.8), channel_id=1, source_target_pairs={{0,8},{8,16},{16,24},{24,0},{1,9},{9,17},{17,25},{25,1},{2,10},{10... | collective-permute-start | bytes 5505032 | tf_op jit(solution)/shard_map/ppermute | solution.py:15
where the time goes:
time: 1090 us; the launch traced here: 1080 us
  waiting for transfers between devices  719 us (66%)
  blocking collectives  185 us (17%)
  matrix products  65.5 us (6%)
  local copies, waits for them, and re-layouts  46 us (4%)
  other arithmetic  44.5 us (4%)
  starting transfers between devices  22.8 us (2%)
    all_to_all x2, waiting for transfers between devices, local(): lax.all_to_all(result.astype(jnp.bfloat16).reshape(sources, slots, featur...  350 us
    all_to_all x1, blocking collectives, local(): lax.all_to_all(send_fwd, 'expert', split_axis=0, concat_axis=0, tiled=True)  185 us
    all_to_all x1, waiting for transfers between devices, local(): lax.all_to_all(send_rows, 'expert', split_axis=0, concat_axis=0, tiled=True)  173 us
    all_to_all x1, waiting for transfers between devices, local(): lax.all_to_all(send_grads, 'expert', split_axis=0, concat_axis=0, tiled=T...  173 us
    ppermute x2, waiting for transfers between devices, from_behind(): lax.ppermute(value, axis, [(i, (i + by) % devices) for i in range(devices)])  22.6 us
  transfers between devices with their start and end apart: 6, of which 5 were waited for; matrix products, arithmetic and copies ran while one was open for 4% of the time, Pallas kernels for 0%

commit v1 on v0

v1 whole, which is shorter than its diff:
```python
import jax
import jax.numpy as jnp
from jax import lax
from jax.sharding import PartitionSpec as P

SHARDS = 4
TOP = 1


EPS = 1e-06


def from_behind(value, axis, by):
    devices = lax.axis_size(axis)
    return lax.ppermute(value, axis, [(i, (i + by) % devices) for i in range(devices)])


def normed(token_rows, gain_row):
    values = token_rows.astype(jnp.float32)
    factor = lax.rsqrt(jnp.mean(values * values, axis=-1, keepdims=True) + EPS)
    return values * factor * gain_row


def slot_tables(route_ids, gate_vals, experts_n, capacity):
    tok_rows, top_n = route_ids.shape
    flat_ids = route_ids.reshape(-1)
    one_hot = (flat_ids[:, None] == jnp.arange(experts_n, dtype=jnp.int32)[None, :]).astype(
        jnp.int32
    )
    slot_ids = jnp.sum((jnp.cumsum(one_hot, axis=0) - one_hot) * one_hot, axis=1)
    position = flat_ids * capacity + slot_ids
    places = jnp.arange(experts_n * capacity, dtype=jnp.int32)
    hit = position[None, :] == places[:, None]
    slot_gate = jnp.sum(jnp.where(hit, gate_vals.reshape(-1)[None, :], jnp.float32(0.0)), axis=1)
    select = jnp.sum(hit.reshape(-1, tok_rows, top_n), axis=2).astype(jnp.bfloat16)
    return select, slot_gate


def pick(select, rows):
    return jnp.dot(select, rows, preferred_element_type=jnp.float32)


def expert_forward(token_rows, gate_cols, up_cols, down_rows):
    pre_gate = jnp.dot(token_rows, gate_cols, preferred_element_type=jnp.float32)
    pre_up = jnp.dot(token_rows, up_cols, preferred_element_type=jnp.float32)
    hidden = (pre_gate * jax.nn.sigmoid(pre_gate) * pre_up).astype(jnp.bfloat16)
    return jnp.dot(hidden, down_rows, preferred_element_type=jnp.float32)


def expert_backward(token_rows, upstream, gate_cols, up_cols, down_rows):
    pre_gate = jnp.dot(token_rows, gate_cols, preferred_element_type=jnp.float32)
    pre_up = jnp.dot(token_rows, up_cols, preferred_element_type=jnp.float32)
    contract = (((1,), (1,)), ((), ()))
    grad_hidden = lax.dot_general(upstream, down_rows, contract, preferred_element_type=jnp.float32)
    sigmoid_gate = jax.nn.sigmoid(pre_gate)
    grad_gate = (
        grad_hidden * pre_up * sigmoid_gate * (1.0 + pre_gate * (1.0 - sigmoid_gate))
    ).astype(jnp.bfloat16)
    grad_up = (grad_hidden * pre_gate * sigmoid_gate).astype(jnp.bfloat16)
    first = lax.dot_general(grad_gate, gate_cols, contract, preferred_element_type=jnp.float32)
    second = lax.dot_general(grad_up, up_cols, contract, preferred_element_type=jnp.float32)
    return first + second


def local(
    acts_fwd,
    routes_fwd,
    gates_fwd,
    stash_bwd,
    grads_bwd,
    routes_bwd,
    gates_bwd,
    gain,
    w_gate,
    w_up,
    w_down,
):
    devices = lax.axis_size("expert")
    experts_n = devices // SHARDS
    tok_rows, features = acts_fwd.shape[1:]
    capacity = min(tok_rows, 9 * tok_rows * TOP // (8 * experts_n))
    gate_cols = w_gate[0]
    up_cols = w_up[0]
    down_rows = w_down[0]
    gain_row = gain[0]
    across = [[e * SHARDS + s for e in range(experts_n)] for s in range(SHARDS)]
    within = [[e * SHARDS + s for s in range(SHARDS)] for e in range(experts_n)]

    def outward(packed):
        swapped = lax.all_to_all(
            packed, "expert", 0, 0, axis_index_groups=across, tiled=True
        )
        return lax.all_gather(swapped, "expert", axis_index_groups=within, axis=0, tiled=True)

    def back(result):
        summed = lax.psum_scatter(
            result, "expert", scatter_dimension=0, axis_index_groups=within, tiled=True
        )
        return lax.all_to_all(summed, "expert", 0, 0, axis_index_groups=across, tiled=True)

    entering = acts_fwd[0]
    select_fwd, unused_gate = slot_tables(routes_fwd[0], gates_fwd[0], experts_n, capacity)
    rows_fwd = pick(select_fwd, normed(entering, gain_row).astype(jnp.bfloat16)).astype(jnp.bfloat16)
    stashed = stash_bwd[0]
    upstream = grads_bwd[0]
    select_bwd, slot_gate = slot_tables(routes_bwd[0], gates_bwd[0], experts_n, capacity)
    rows_bwd = pick(select_bwd, normed(stashed, gain_row).astype(jnp.bfloat16)).astype(jnp.bfloat16)
    rows_grad = (pick(select_bwd, upstream) * slot_gate[:, None]).astype(jnp.bfloat16)
    all_fwd = outward(rows_fwd)
    all_bwd = outward(rows_bwd)
    all_grad = outward(rows_grad)
    result = expert_forward(all_fwd, gate_cols, up_cols, down_rows).astype(jnp.bfloat16)
    back_fwd = back(result)
    result = expert_backward(all_bwd, all_grad, gate_cols, up_cols, down_rows).astype(jnp.bfloat16)
    back_bwd = back(result)
    mixture = gates_fwd[0] * pick(select_fwd.T, back_fwd)
    layer_out = (entering.astype(jnp.float32) + mixture).astype(jnp.bfloat16)
    grad_normed = pick(select_bwd.T, back_bwd)

    def norm_only(values):
        return normed(values, gain_row)

    unused, pullback = jax.vjp(norm_only, stashed.astype(jnp.float32))
    grad_input = (upstream.astype(jnp.float32) + pullback(grad_normed)[0]).astype(jnp.bfloat16)
    fwd_next = from_behind(layer_out[None], "section", 1)
    grad_next = from_behind(grad_input[None], "section", -1)
    return (fwd_next, grad_next)


def solution(mesh):
    return jax.shard_map(
        local,
        mesh=mesh,
        in_specs=(
            P("section", "expert", None),
            P("section", "expert", None),
            P("section", "expert", None),
            P("section", "expert", None),
            P("section", "expert", None),
            P("section", "expert", None),
            P("section", "expert", None),
            P("section", None),
            P("section", None, "expert"),
            P("section", None, "expert"),
            P("section", "expert", None),
        ),
        out_specs=(P("section", "expert", None), P("section", "expert", None)),
        check_vma=False,
    )
```

time: 1090 us -> 879 us (0.81)
  waiting for transfers between devices: 719 us -> 606 us
  local copies, waits for them, and re-layouts: 46 us -> 2.49 us
  other arithmetic: 44.5 us -> 8.33 us
  blocking collectives: 185 us -> 153 us
  matrix products: 65.5 us -> 82.9 us
  between operations: 1.08 us -> 14 us
  starting transfers between devices: 22.8 us -> 11.1 us
    all_to_all x4 -> x2, waiting for transfers between devices: 696 us -> 41.9 us  [back(): lax.all_to_all(summed, 'expert', 0, 0, axis_index_groups=across, tiled=True)]
    all_gather x0 -> x3, waiting for transfers between devices: none -> 283 us  [outward(): lax.all_gather(swapped, 'expert', axis_index_groups=within, axis=0, tiled...]
    reduce_scatter x0 -> x2, waiting for transfers between devices: none -> 258 us  [back(): lax.psum_scatter(result, 'expert', scatter_dimension=0, axis_index_groups...]
    all_to_all x1 -> x3, blocking collectives: 185 us -> 153 us  [outward(): lax.all_to_all(packed, 'expert', 0, 0, axis_index_groups=across, tiled=True)]
    gather x5 -> x0, local copies, waits for them, and re-layouts: 27.7 us -> none  [the longest x2 9.99 us: pack_rows(): picked = jnp.take(token_rows, owner, axis=0)]
    reduce_sum x5 -> x0, other arithmetic: 20.2 us -> none  [the longest x2 14.4 us: unfold_shards(): return jnp.sum(grouped, axis=1).reshape(experts_n * slots, features)]
    convert_element_type x4 -> x0, other arithmetic: 13.4 us -> none  [the longest x1 5.11 us: local(): (upstream.astype(jnp.float32) + pullback(grad_normed)[0]).astype(jnp.bflo...]
    all_to_all x4 -> x2, starting transfers between devices: 22.6 us -> 9.68 us  [back(): lax.all_to_all(summed, 'expert', 0, 0, axis_index_groups=across, tiled=True)]
  transfers between devices with their start and end apart: 6 -> 9, of which waited for: 5 -> 7; matrix products, arithmetic and copies ran while one was open for 4% -> 10% of each run, Pallas kernels for 0% -> 0%
where the time goes in v1:
time: 879 us; the launch traced here: 878 us
  waiting for transfers between devices  606 us (69%)
  blocking collectives  153 us (17%)
  matrix products  82.9 us (9%)
  between operations  14 us (2%)
  starting transfers between devices  11.1 us (1%)
    all_gather x3, waiting for transfers between devices, outward(): lax.all_gather(swapped, 'expert', axis_index_groups=within, axis=0, tiled...  283 us
    reduce_scatter x2, waiting for transfers between devices, back(): lax.psum_scatter(result, 'expert', scatter_dimension=0, axis_index_groups...  258 us
    all_to_all x3, blocking collectives, outward(): lax.all_to_all(packed, 'expert', 0, 0, axis_index_groups=across, tiled=True)  153 us
    all_to_all x2, waiting for transfers between devices, back(): lax.all_to_all(summed, 'expert', 0, 0, axis_index_groups=across, tiled=True)  41.9 us
    ppermute x2, waiting for transfers between devices, from_behind(): lax.ppermute(value, axis, [(i, (i + by) % devices) for i in range(devices)])  22.6 us
    dot_general x1, matrix products, expert_backward(): lax.dot_general(grad_gate, gate_cols, contract, preferred_element_type=jn...  21.5 us
    dot_general x1, matrix products, expert_forward(): return jnp.dot(hidden, down_rows, preferred_element_type=jnp.float32)  17.9 us
  transfers between devices with their start and end apart: 9, of which 7 were waited for; matrix products, arithmetic and copies ran while one was open for 10% of the time, Pallas kernels for 0%

profile of v1, /device:TPU:0, one launch (start us, length us, event | category | flops | bytes accessed | tf_op | source)
XLA Modules:
  0.0 878.0 jit_solution(8964202946865359607)
XLA Ops:
  7.2 0.0 all-gather.6.cloned.1.call-start
  7.2 0.7 fusion.74
  8.0 0.2 reduce_window_sum.18
  8.1 0.8 select_reduce_fusion.1
  9.0 0.7 multiply_add_fusion.1
  9.6 0.8 select_reduce_fusion
  10.4 2.2 fusion.1
  12.6 0.0 copy-start
  12.6 0.0 copy-start.2
  12.6 52.8 %all_to_all.60 = bf16[2,72,7168]{2,1,0:T(8,128)(2,1)} all-to-all(bf16[2,72,7168]{2,1,0:T(8,128)(2,1)S(1)} %bitcast.112), channel_id=1, replica_groups={{0,4},{1,5},{2,6},{3,7},{8,12},{9,13},{10,14},{11,15},{16,20},{17,21},{..., dimensions={0} | all-to-all | bytes 4128768 | tf_op jit(solution)/shard_map/all_to_all | solution.py:90
  65.5 0.0 all-gather.6.cloned.1.call-update
  65.5 0.0 all-gather.8.cloned.1.call-start
  65.5 0.0 copy-done
  65.5 0.4 fusion.8
  66.0 0.0 copy-done.2
  66.0 0.8 convolution_convert_fusion.1
  66.8 0.0 copy-start.3
  66.8 50.0 %all_to_all.61 = bf16[2,72,7168]{2,1,0:T(8,128)(2,1)} all-to-all(bf16[2,72,7168]{2,1,0:T(8,128)(2,1)S(1)} %bitcast.114), channel_id=1, replica_groups={{0,4},{1,5},{2,6},{3,7},{8,12},{9,13},{10,14},{11,15},{16,20},{17,21},{..., dimensions={0} | all-to-all | bytes 4128768 | tf_op jit(solution)/shard_map/all_to_all | solution.py:90
  116.8 0.0 all-gather.8.cloned.1.call-update
  116.8 0.0 all-gather.4.cloned.1.call-start
  116.9 0.0 copy-done.3
  116.9 0.1 fusion.75
  117.0 0.2 reduce_window_sum.17
  117.2 0.2 select_reduce_fusion.2
  117.3 1.9 fusion.12
  119.3 2.3 convolution_convert_fusion.2
  121.6 50.2 %all_to_all.62 = bf16[2,72,7168]{2,1,0:T(8,128)(2,1)} all-to-all(bf16[2,72,7168]{2,1,0:T(8,128)(2,1)S(1)} %bitcast.113), channel_id=1, replica_groups={{0,4},{1,5},{2,6},{3,7},{8,12},{9,13},{10,14},{11,15},{16,20},{17,21},{..., dimensions={0} | all-to-all | bytes 4128768 | tf_op jit(solution)/shard_map/all_to_all | solution.py:90
  171.8 0.0 all-gather.4.cloned.1.call-update
  171.8 0.2 reduce-scatter.5.cloned.1.call-start
  172.0 38.0 %all-gather.6.cloned.1.call-done = bf16[576,7168]{1,0:T(8,128)(2,1)} async-done(((bf16[144,7168]{1,0:T(8,128)(2,1)}), bf16[576,7168]{1,0:T(8,128)(2,1)}) %all-gather.6.cloned.1.call-update) | async-done | bytes 8257552 | tf_op jit(solution)/shard_map/all_gather | solution.py:93
  210.0 6.7 fusion.17
  216.7 140.0 %all-gather.8.cloned.1.call-done = bf16[576,7168]{1,0:T(8,128)(2,1)} async-done(((bf16[144,7168]{1,0:T(8,128)(2,1)}), bf16[576,7168]{1,0:T(8,128)(2,1)}) %all-gather.8.cloned.1.call-update) | async-done | bytes 8257552 | tf_op jit(solution)/shard_map/all_gather | solution.py:93
  356.7 6.7 fusion.27
  363.4 21.5 %fusion.25 = f32[576,7168]{1,0:T(8,128)} fusion(bf16[1,7168,256]{2,1,0:T(8,128)(2,1)} %param.19, f32[576,256]{1,0:T(8,128)S(1)} %fusion.17, bf16[576,7168]{1,0:T(8,128)(2,1)} %all-gather.8.cloned.1.call-done, bf16[1,7168,256]{2,1,0:T(8,128)(2,1)} %param.20, f32[576,256]{1,0:T(8,128)S(1)} %fusion.27), kind=kOutput, calls=%fused_computation.37 | convolution fusion | flops 4229332992 | bytes 33292288 | tf_op jit(solution)/shard_map/dot_general | solution.py:60
  384.9 12.6 %add_convert_fusion = bf16[576,7168]{1,0:T(8,128)(2,1)} fusion(f32[576,7168]{1,0:T(8,128)} %fusion.25, bf16[1,7168,256]{2,1,0:T(8,128)(2,1)} %param.20, f32[576,256]{1,0:T(8,128)S(1)} %fusion.17, f32[576,256]{1,0:T(8,128)S(1)} %fusion.27), kind=kOutput, calls=%fused_computation | convolution fusion | flops 2123071488 | bytes 29622272 | tf_op jit(solution)/shard_map/dot_general | solution.py:61
  397.5 0.0 reduce-scatter.5.cloned.1.call-update
  397.5 0.0 reduce-scatter.3.cloned.1.call-start
  397.6 105.4 %all-gather.4.cloned.1.call-done = bf16[576,7168]{1,0:T(8,128)(2,1)} async-done(((bf16[144,7168]{1,0:T(8,128)(2,1)}), bf16[576,7168]{1,0:T(8,128)(2,1)}) %all-gather.4.cloned.1.call-update) | async-done | bytes 8257552 | tf_op jit(solution)/shard_map/all_gather | solution.py:93
  502.9 6.7 fusion.29
  509.6 17.9 %convolution_convert_fusion = bf16[576,7168]{1,0:T(8,128)(2,1)} fusion(bf16[1,256,7168]{2,1,0:T(8,128)(2,1)} %param.21, bf16[576,7168]{1,0:T(8,128)(2,1)} %all-gather.4.cloned.1.call-done, bf16[1,7168,256]{2,1,0:T(8,128)(2,1)} %param.20, f32[576,256]{1,0:T(8,128)S(1)} %fusion.29), kind=kOutput, calls=%fused_computation.1 | convolution fusion | flops 4232871936 | bytes 24444928 | tf_op jit(solution)/shard_map/dot_general | solution.py:47
  527.5 0.0 reduce-scatter.3.cloned.1.call-update
  527.6 118.8 %reduce-scatter.5.cloned.1.call-done = bf16[144,7168]{1,0:T(8,128)(2,1)} async-done(((bf16[576,7168]{1,0:T(8,128)(2,1)}), bf16[144,7168]{1,0:T(8,128)(2,1)}) %reduce-scatter.5.cloned.1.call-update) | async-done | bytes 2064400 | tf_op jit(solution)/shard_map/reduce_scatter | solution.py:96
  646.3 4.9 all-to-all-start.4
  651.2 139.5 %reduce-scatter.3.cloned.1.call-done = bf16[144,7168]{1,0:T(8,128)(2,1)} async-done(((bf16[576,7168]{1,0:T(8,128)(2,1)}), bf16[144,7168]{1,0:T(8,128)(2,1)}) %reduce-scatter.3.cloned.1.call-update) | async-done | bytes 2064400 | tf_op jit(solution)/shard_map/reduce_scatter | solution.py:96
  790.7 0.0 all-to-all-done.4
  790.7 4.8 all-to-all-start.1
  795.5 0.0 copy-start.1
  795.5 2.6 fusion.9
  798.2 0.0 copy-done.1
  798.2 0.0 copy-start.4
  798.2 2.3 fusion.31
  800.5 1.0 collective-permute-start.1
  801.5 41.9 %all-to-all-done.1 = bf16[2,72,7168]{2,1,0:T(8,128)(2,1)} async-done(((bf16[2,72,7168]{2,1,0:T(8,128)(2,1)}), bf16[2,72,7168]{2,1,0:T(8,128)(2,1)}, u32[]{:S(2)}, u32[]{:S(2)}) %all-to-all-start.1) | async-done | bytes 2064416 | tf_op jit(solution)/shard_map/all_to_all | solution.py:99
  843.4 0.0 copy-done.4
  843.5 2.9 fusion.3
  846.3 0.1 collective-permute-start
  846.4 0.0 collective-permute-done.1
  846.4 22.6 %collective-permute-done = bf16[1,128,7168]{2,1,0:T(8,128)(2,1)S(1)} collective-permute-done((bf16[1,128,7168]{2,1,0:T(8,128)(2,1)S(1)}, bf16[1,128,7168]{2,1,0:T(8,128)(2,1)S(1)}, u32[]{:S(2)}, u32[]{:S(2)}) %collective-permute-start) | collective-permute-done | bytes 1835040 | tf_op jit(solution)/shard_map/ppermute | solution.py:15
  869.0 1.2 copy.15
  870.3 1.2 copy.16
  (4 shorter events, 0.0 us)
Async XLA Ops:
  7.2 202.8 %all-gather.6.cloned.1.call-start = ((), (), s32[]{:S(2)}) async-start(), calls=%async_computation.9 | async-start | bytes 10321920 | tf_op jit(solution)/shard_map/all_gather | solution.py:93
  12.6 52.9 %copy-start = (bf16[1,128,7168]{2,1,0:T(8,128)(2,1)S(1)}, bf16[1,128,7168]{2,1,0:T(8,128)(2,1)}, u32[]{:S(2)}) copy-start(bf16[1,128,7168]{2,1,0:T(8,128)(2,1)} %param.14) | copy-start | bytes 5505028
  12.6 53.4 %copy-start.2 = (f32[1,7168]{1,0:T(1,128)S(1)}, f32[1,7168]{1,0:T(1,128)}, u32[]{:S(2)}) copy-start(f32[1,7168]{1,0:T(1,128)} %param.18) | copy-start | bytes 86020
  65.5 291.2 %all-gather.8.cloned.1.call-start = ((), (), s32[]{:S(2)}) async-start(), calls=%async_computation.10 | async-start | bytes 10321920 | tf_op jit(solution)/shard_map/all_gather | solution.py:93
  66.8 50.1 %copy-start.3 = (s32[1,128,1]{1,2,0:T(1,128)S(1)}, s32[1,128,1]{1,2,0:T(1,128)}, u32[]{:S(2)}) copy-start(s32[1,128,1]{1,2,0:T(1,128)} %param.12) | copy-start | bytes 1540
  116.8 386.1 %all-gather.4.cloned.1.call-start = ((), (), s32[]{:S(2)}) async-start(), calls=%async_computation.7 | async-start | bytes 10321920 | tf_op jit(solution)/shard_map/all_gather | solution.py:93
  171.8 474.5 %reduce-scatter.5.cloned.1.call-start = ((), (), s32[]{:S(2)}) async-start(), calls=%async_computation.11 | async-start | bytes 10321920 | tf_op jit(solution)/shard_map/reduce_scatter | solution.py:96
  397.5 393.2 %reduce-scatter.3.cloned.1.call-start = ((), (), s32[]{:S(2)}) async-start(), calls=%async_computation.8 | async-start | bytes 10321920 | tf_op jit(solution)/shard_map/reduce_scatter | solution.py:96
  646.3 144.4 %all-to-all-start.4 = ((bf16[2,72,7168]{2,1,0:T(8,128)(2,1)}), bf16[2,72,7168]{2,1,0:T(8,128)(2,1)}, u32[]{:S(2)}, u32[]{:S(2)}) async-start(bf16[2,72,7168]{2,1,0:T(8,128)(2,1)} %bitcast.119), calls=%async_computation.6 | async-start | bytes 4128768 | tf_op jit(solution)/shard_map/all_to_all | solution.py:99
  790.7 52.7 %all-to-all-start.1 = ((bf16[2,72,7168]{2,1,0:T(8,128)(2,1)}), bf16[2,72,7168]{2,1,0:T(8,128)(2,1)}, u32[]{:S(2)}, u32[]{:S(2)}) async-start(bf16[2,72,7168]{2,1,0:T(8,128)(2,1)} %bitcast.118), calls=%async_computation.2 | async-start | bytes 4128768 | tf_op jit(solution)/shard_map/all_to_all | solution.py:99
  795.5 2.7 copy-start.1
  798.2 45.2 %copy-start.4 = (f32[1,128,1]{1,2,0:T(1,128)S(1)}, f32[1,128,1]{1,2,0:T(1,128)}, u32[]{:S(2)}) copy-start(f32[1,128,1]{1,2,0:T(1,128)} %param.13) | copy-start | bytes 1540
  800.5 45.9 %collective-permute-start.1 = (bf16[1,128,7168]{2,1,0:T(8,128)(2,1)}, bf16[1,128,7168]{2,1,0:T(8,128)(2,1)S(1)}, u32[]{:S(2)}, u32[]{:S(2)}) collective-permute-start(bf16[1,128,7168]{2,1,0:T(8,128)(2,1)} %fusion.31), channel_id=1, source_target_pairs={{0,24},{8,0},{16,8},{24,16},{1,25},{9,1},{17,9},{25,17},{2,26},{10... | collective-permute-start | bytes 5505032 | tf_op jit(solution)/shard_map/ppermute | solution.py:15
  846.3 22.7 %collective-permute-start = (bf16[1,128,7168]{2,1,0:T(8,128)(2,1)S(1)}, bf16[1,128,7168]{2,1,0:T(8,128)(2,1)S(1)}, u32[]{:S(2)}, u32[]{:S(2)}) collective-permute-start(bf16[1,128,7168]{2,1,0:T(8,128)(2,1)S(1)} %fusion.3), channel_id=1, source_target_pairs={{0,8},{8,16},{16,24},{24,0},{1,9},{9,17},{17,25},{25,1},{2,10},{10... | collective-permute-start | bytes 5505032 | tf_op jit(solution)/shard_map/ppermute | solution.py:15
Sparse Core Ops, SparseCore 0:
  65.6 144.3 all-gather.5
  211.6 145.1 all-gather.7
  358.3 144.6 all-gather.3
  505.2 141.1 reduce-scatter.4
  648.7 141.9 reduce-scatter.2

commit v2 on v1

--- a/solution.py
+++ b/solution.py
@@ -1,6 +1,10 @@
+import functools
+
 import jax
 import jax.numpy as jnp
 from jax import lax
+from jax.experimental import pallas as pl
+from jax.experimental.pallas import tpu as pltpu
 from jax.sharding import PartitionSpec as P
 
 SHARDS = 4
@@ -60,6 +64,295 @@
     first = lax.dot_general(grad_gate, gate_cols, contract, preferred_element_type=jnp.float32)
     second = lax.dot_general(grad_up, up_cols, contract, preferred_element_type=jnp.float32)
     return first + second
+
+
+MESH = pl.DeviceIdType.MESH
+VMEM_BYTES = 58 * 1024 * 1024
+
+
+def swap_last(position):
+    return position + (position // 2) * (1 - 2 * (position % 2))
+
+
+def ring_shard(position, experts_n):
+    position = position % SHARDS
+    return swap_last(position) if experts_n == 2 else position
+
+
+def places(experts_n):
+    me = lax.axis_index("expert")
+    group, shard = me // SHARDS, me % SHARDS
+    position = swap_last(shard) if experts_n == 2 else shard
+    right = ring_shard(position + 1, experts_n)
+    far = ring_shard(position + 2, experts_n)
+    left = ring_shard(position + 3, experts_n)
+    return group, shard, left, right, far
+
+
+def greet(experts_n, group, shard, left, right):
+    barrier = pltpu.get_barrier_semaphore()
+    partners = [group * SHARDS + left, group * SHARDS + right]
+    for step in range(1, experts_n):
+        partners.append((group + step) % experts_n * SHARDS + shard)
+    for partner in partners:
+        pl.semaphore_signal(barrier, inc=1, device_id={"expert": partner}, device_id_type=MESH)
+    pl.semaphore_wait(barrier, len(partners))
+
+
+def remote(src, dst, send, recv, target):
+    return pltpu.make_async_remote_copy(
+        src_ref=src,
+        dst_ref=dst,
+        send_sem=send,
+        recv_sem=recv,
+        device_id={"expert": target},
+        device_id_type=MESH,
+    )
+
+
+def outward_kernel(experts_n, arrays, *refs):
+    packed, gathered = refs[:arrays], refs[arrays : 2 * arrays]
+    cross_send, cross_recv, ring_send, ring_recv, half_send, half_recv, local_sem = refs[2 * arrays :]
+    group, shard, left, right, far = places(experts_n)
+    greet(experts_n, group, shard, left, right)
+    half = packed[0].shape[2] // 2
+    sides = ((right, left), (left, right))
+    started = []
+
+    def begin(copy):
+        copy.start()
+        started.append(copy)
+        return copy
+
+    crossing, ring, local = {}, {}, []
+    for a in range(arrays):
+        for step in range(1, experts_n):
+            expert = (group + step) % experts_n
+            crossing[a, step] = begin(
+                remote(
+                    packed[a].at[expert],
+                    gathered[a].at[group, shard],
+                    cross_send.at[a, step],
+                    cross_recv.at[a, step],
+                    expert * SHARDS + shard,
+                )
+            )
+        for side, (target, unused) in enumerate(sides):
+            ring[a, 0, side] = begin(
+                remote(
+                    packed[a].at[group],
+                    gathered[a].at[group, shard],
+                    ring_send.at[a, 0, side],
+                    ring_recv.at[a, 0, side],
+                    group * SHARDS + target,
+                )
+            )
+        copy = pltpu.make_async_copy(
+            packed[a].at[group], gathered[a].at[group, shard], local_sem.at[a]
+        )
+        copy.start()
+        local.append(copy)
+
+    def relay(a, step):
+        origin = (group + experts_n - step) % experts_n
+        for side, (target, source) in enumerate(sides):
+            ring[a, step, side].wait_recv()
+            block = gathered[a].at[origin, source, :, pl.ds(side * half, half)]
+            halves[a, step, side] = begin(
+                remote(
+                    block,
+                    block,
+                    half_send.at[a, step, side],
+                    half_recv.at[a, step, side],
+                    group * SHARDS + target,
+                )
+            )
+
+    halves = {}
+    for a in range(arrays):
+        for step in range(1, experts_n):
+            origin = (group + experts_n - step) % experts_n
+            crossing[a, step].wait_recv()
+            block = gathered[a].at[origin, shard]
+            for side, (target, unused) in enumerate(sides):
+                ring[a, step, side] = begin(
+                    remote(
+                        block,
+                        block,
+                        ring_send.at[a, step, side],
+                        ring_recv.at[a, step, side],
+                        group * SHARDS + target,
+                    )
+                )
+        relay(a, 0)
+        if a > 0:
+            for step in range(1, experts_n):
+                relay(a - 1, step)
+    for step in range(1, experts_n):
+        relay(arrays - 1, step)
+    for copy in halves.values():
+        copy.wait_recv()
+    for copy in local:
+        copy.wait()
+    for copy in started:
+        copy.wait_send()
+
+
+def outward_call(packed, experts_n):
+    arrays = len(packed)
+    unused, capacity, features = packed[0].shape
+    dma = pltpu.SemaphoreType.DMA
+    shape = jax.ShapeDtypeStruct((experts_n, SHARDS, capacity, features), jnp.bfloat16)
+    return pl.pallas_call(
+        functools.partial(outward_kernel, experts_n, arrays),
+        out_shape=[shape] * arrays,
+        in_specs=[pl.BlockSpec(memory_space=pl.ANY)] * arrays,
+        out_specs=[pl.BlockSpec(memory_space=pl.ANY)] * arrays,
+        scratch_shapes=[
+            dma((arrays, experts_n)),
+            dma((arrays, experts_n)),
+            dma((arrays, experts_n, 2)),
+            dma((arrays, experts_n, 2)),
+            dma((arrays, experts_n, 2)),
+            dma((arrays, experts_n, 2)),
+            dma((arrays,)),
+        ],
+        compiler_params=pltpu.CompilerParams(
+            collective_id=0, has_side_effects=True, vmem_limit_bytes=VMEM_BYTES
+        ),
+        name="rows_to_experts",
+    )(*packed)
+
+
+def add_into(dst, terms, columns):
+    tile = 512 if columns % 512 == 0 else 128
+
+    @pl.loop(0, columns // tile)
+    def _(i):
+        at = pl.ds(pl.multiple_of(i * tile, tile), tile)
+        total = terms[0][:, at].astype(jnp.float32)
+        for term in terms[1:]:
+            total = total + term[:, at].astype(jnp.float32)
+        dst[:, at] = total.astype(dst.dtype)
+
+
+def return_kernel(experts_n, arrays, *refs):
+    partial, summed = refs[:arrays], refs[arrays : 2 * arrays]
+    far_in, near_in, total, far_send, far_recv, near_send, near_recv, out_send, out_recv, local_sem = refs[
+        2 * arrays :
+    ]
+    group, shard, left, right, far = places(experts_n)
+    greet(experts_n, group, shard, left, right)
+    half = partial[0].shape[3] // 2
+    sides = ((right, left), (left, right))
+    cols = (pl.ds(0, half), pl.ds(half, half))
+    started, far_copies, near_copies, out_copies, local = [], {}, {}, {}, []
+
+    def begin(copy):
+        copy.start()
+        started.append(copy)
+        return copy
+
+    order = [(a, step) for a in range(arrays) for step in list(range(1, experts_n)) + [0]]
+    for a, step in order:
+        origin = (group + step) % experts_n
+        for side, (target, unused) in enumerate(sides):
+            far_copies[a, step, side] = begin(
+                remote(
+                    partial[a].at[origin, far, :, cols[side]],
+                    far_in.at[a, step, side],
+                    far_send.at[a, step, side],
+                    far_recv.at[a, step, side],
+                    group * SHARDS + target,
+                )
+            )
+    for a, step in order:
+        origin = (group + step) % experts_n
+        for side, (target, unused) in enumerate(sides):
+            near_copies[a, step, side, 1] = begin(
+                remote(
+                    partial[a].at[origin, target, :, cols[1 - side]],
+                    near_in.at[a, step, side, :, cols[1 - side]],
+                    near_send.at[a, step, side, 1],
+                    near_recv.at[a, step, side, 1],
+                    group * SHARDS + target,
+                )
+            )
+    for a, step in order:
+        origin = (group + step) % experts_n
+        for side, (target, unused) in enumerate(sides):
+            far_copies[a, step, side].wait_recv()
+            block = far_in.at[a, step, side]
+            add_into(block, (block, partial[a].at[origin, target, :, cols[side]]), half)
+            near_copies[a, step, side, 0] = begin(
+                remote(
+                    block,
+                    near_in.at[a, step, side, :, cols[side]],
+                    near_send.at[a, step, side, 0],
+                    near_recv.at[a, step, side, 0],
+                    group * SHARDS + target,
+                )
+            )
+    for a, step in order:
+        origin = (group + step) % experts_n
+        for side in range(2):
+            for part in range(2):
+                near_copies[a, step, side, part].wait_recv()
+        result = total.at[a, step]
+        add_into(
+            result,
+            (near_in.at[a, step, 0], near_in.at[a, step, 1], partial[a].at[origin, shard]),
+            2 * half,
+        )
+        if step == 0:
+            copy = pltpu.make_async_copy(result, summed[a].at[group], local_sem.at[a])
+            copy.start()
+            local.append(copy)
+        else:
+            out_copies[a, step] = begin(
+                remote(
+                    result,
+                    summed[a].at[group],
+                    out_send.at[a, step],
+                    out_recv.at[a, step],
+                    origin * SHARDS + shard,
+                )
+            )
+    for copy in out_copies.values():
+        copy.wait_recv()
+    for copy in local:
+        copy.wait()
+    for copy in started:
+        copy.wait_send()
+
+
+def return_call(partial):
+    arrays = len(partial)
+    experts_n, unused, capacity, features = partial[0].shape
+    dma = pltpu.SemaphoreType.DMA
+    shape = jax.ShapeDtypeStruct((experts_n, capacity, features), jnp.bfloat16)
+    return pl.pallas_call(
+        functools.partial(return_kernel, experts_n, arrays),
+        out_shape=[shape] * arrays,
+        in_specs=[pl.BlockSpec(memory_space=pltpu.VMEM)] * arrays,
+        out_specs=[pl.BlockSpec(memory_space=pl.ANY)] * arrays,
+        scratch_shapes=[
+            pltpu.VMEM((arrays, experts_n, 2, capacity, features // 2), jnp.bfloat16),
+            pltpu.VMEM((arrays, experts_n, 2, capacity, features), jnp.bfloat16),
+            pltpu.VMEM((arrays, experts_n, capacity, features), jnp.bfloat16),
+            dma((arrays, experts_n, 2)),
+            dma((arrays, experts_n, 2)),
+            dma((arrays, experts_n, 2, 2)),
+            dma((arrays, experts_n, 2, 2)),
+            dma((arrays, experts_n)),
+            dma((arrays, experts_n)),
+            dma((arrays,)),
+        ],
+        compiler_params=pltpu.CompilerParams(
+            collective_id=1, has_side_effects=True, vmem_limit_bytes=VMEM_BYTES
+        ),
+        name="sums_to_tokens",
+    )(*partial)
 
 
 def local(
@@ -83,21 +376,6 @@
     up_cols = w_up[0]
     down_rows = w_down[0]
     gain_row = gain[0]
-    across = [[e * SHARDS + s for e in range(experts_n)] for s in range(SHARDS)]
-    within = [[e * SHARDS + s for s in range(SHARDS)] for e in range(experts_n)]
-
-    def outward(packed):
-        swapped = lax.all_to_all(
-            packed, "expert", 0, 0, axis_index_groups=across, tiled=True
-        )
-        return lax.all_gather(swapped, "expert", axis_index_groups=within, axis=0, tiled=True)
-
-    def back(result):
-        summed = lax.psum_scatter(
-            result, "expert", scatter_dimension=0, axis_index_groups=within, tiled=True
-        )
-        return lax.all_to_all(summed, "expert", 0, 0, axis_index_groups=across, tiled=True)
-
     entering = acts_fwd[0]
     select_fwd, unused_gate = slot_tables(routes_fwd[0], gates_fwd[0], experts_n, capacity)
     rows_fwd = pick(select_fwd, normed(entering, gain_row).astype(jnp.bfloat16)).astype(jnp.bfloat16)
@@ -106,13 +384,21 @@
     select_bwd, slot_gate = slot_tables(routes_bwd[0], gates_bwd[0], experts_n, capacity)
     rows_bwd = pick(select_bwd, normed(stashed, gain_row).astype(jnp.bfloat16)).astype(jnp.bfloat16)
     rows_grad = (pick(select_bwd, upstream) * slot_gate[:, None]).astype(jnp.bfloat16)
-    all_fwd = outward(rows_fwd)
-    all_bwd = outward(rows_bwd)
-    all_grad = outward(rows_grad)
-    result = expert_forward(all_fwd, gate_cols, up_cols, down_rows).astype(jnp.bfloat16)
-    back_fwd = back(result)
-    result = expert_backward(all_bwd, all_grad, gate_cols, up_cols, down_rows).astype(jnp.bfloat16)
-    back_bwd = back(result)
+    packed = [
+        rows.reshape(experts_n, capacity, features) for rows in (rows_fwd, rows_bwd, rows_grad)
+    ]
+    all_fwd, all_bwd, all_grad = [
+        rows.reshape(-1, features) for rows in outward_call(packed, experts_n)
+    ]
+    results = (
+        expert_forward(all_fwd, gate_cols, up_cols, down_rows),
+        expert_backward(all_bwd, all_grad, gate_cols, up_cols, down_rows),
+    )
+    partial = [
+        result.astype(jnp.bfloat16).reshape(experts_n, SHARDS, capacity, features)
+        for result in results
+    ]
+    back_fwd, back_bwd = [rows.reshape(-1, features) for rows in return_call(partial)]
     mixture = gates_fwd[0] * pick(select_fwd.T, back_fwd)
     layer_out = (entering.astype(jnp.float32) + mixture).astype(jnp.bfloat16)
     grad_normed = pick(select_bwd.T, back_bwd)

time: 879 us -> 597 us (0.68)
  waiting for transfers between devices: 606 us -> 40.6 us
  Pallas kernels: 0 us -> 470 us
  blocking collectives: 153 us -> 0 us
  between operations: 14 us -> 0.9 us
  starting transfers between devices: 11.1 us -> 0.12 us
  matrix products: 82.9 us -> 73.8 us
    pallas_call x0 -> x2, Pallas kernels: none -> 470 us  [the longest x1 272 us: outward_call(): pl.pallas_call(functools.partial(outward_kernel, experts_n, arrays), out_...]
    all_gather x3 -> x0, waiting for transfers between devices: 283 us -> none  [outward(): lax.all_gather(swapped, 'expert', axis_index_groups=within, axis=0, tiled...]
    reduce_scatter x2 -> x0, waiting for transfers between devices: 258 us -> none  [back(): lax.psum_scatter(result, 'expert', scatter_dimension=0, axis_index_groups...]
    all_to_all x3 -> x0, blocking collectives: 153 us -> none  [outward(): lax.all_to_all(packed, 'expert', 0, 0, axis_index_groups=across, tiled=True)]
    all_to_all x2 -> x0, waiting for transfers between devices: 41.9 us -> none  [back(): lax.all_to_all(summed, 'expert', 0, 0, axis_index_groups=across, tiled=True)]
    ppermute x2, waiting for transfers between devices: 22.6 us -> 40.6 us  [from_behind(): lax.ppermute(value, axis, [(i, (i + by) % devices) for i in range(devices)])]
    all_to_all x2 -> x0, starting transfers between devices: 9.68 us -> none  [back(): lax.all_to_all(summed, 'expert', 0, 0, axis_index_groups=across, tiled=True)]
  transfers between devices with their start and end apart: 9 -> 2, of which waited for: 7 -> 2; matrix products, arithmetic and copies ran while one was open for 10% -> 0% of each run, Pallas kernels for 0% -> 0%
where the time goes in v2:
time: 597 us
  Pallas kernels  470 us (79%)
  matrix products  73.8 us (12%)
  waiting for transfers between devices  40.6 us (7%)
  other arithmetic  6.09 us (1%)
    pallas_call x1, Pallas kernels, outward_call(): pl.pallas_call(functools.partial(outward_kernel, experts_n, arrays), out_...  272 us
    pallas_call x1, Pallas kernels, return_call(): pl.pallas_call(functools.partial(return_kernel, experts_n, arrays), out_s...  198 us
    ppermute x2, waiting for transfers between devices, from_behind(): lax.ppermute(value, axis, [(i, (i + by) % devices) for i in range(devices)])  40.6 us
    dot_general x1, matrix products, expert_backward(): lax.dot_general(grad_gate, gate_cols, contract, preferred_element_type=jn...  19.8 us
    dot_general x1, matrix products, expert_forward(): return jnp.dot(hidden, down_rows, preferred_element_type=jnp.float32)  17.8 us
    dot_general x1, matrix products, expert_backward(): lax.dot_general(grad_up, up_cols, contract, preferred_element_type=jnp.fl...  12.6 us
  transfers between devices with their start and end apart: 2, of which 2 were waited for; matrix products, arithmetic and copies ran while one was open for 0% of the time, Pallas kernels for 0%

profile of v2, /device:TPU:0, one launch (start us, length us, event | category | flops | bytes accessed | tf_op | source)
XLA Modules:
  0.0 597.0 jit_solution(9424101352606478853)
XLA Ops:
  0.6 0.0 copy-start
  0.6 0.0 copy-start.9
  0.7 0.0 copy-start.10
  0.7 0.0 copy-start.12
  0.7 0.0 copy-start.8
  0.7 2.1 fusion.8
  2.8 1.9 fusion.12
  4.7 0.0 copy-done.9
  4.7 0.1 fusion.75
  4.8 0.2 reduce_window_sum.17
  5.0 0.2 select_reduce_fusion.2
  5.2 0.0 copy-done.10
  5.2 0.1 fusion.74
  5.3 0.2 reduce_window_sum.18
  5.4 0.2 select_reduce_fusion.1
  5.6 0.0 copy-done.12
  5.6 0.1 select_reduce_fusion
  5.8 0.0 copy-start.1
  5.8 3.7 fusion.1
  9.5 0.0 copy-done
  9.5 0.0 copy-done.8
  9.5 2.1 convolution_convert_fusion.1
  11.6 0.0 copy-done.1
  11.6 2.2 convolution_convert_fusion.2
  13.7 272.4 %rows_to_experts.1 = (bf16[2,4,72,7168]{3,2,1,0:T(8,128)(2,1)}, bf16[2,4,72,7168]{3,2,1,0:T(8,128)(2,1)}, bf16[2,4,72,7168]{3,2,1,0:T(8,128)(2,1)}) custom-call(bf16[2,72,7168]{2,1,0:T(8,128)(2,1)} %bitcast.120, bf16[2,72,7168]{2,1,0:T(8,128)(2,1)} %bitcast.119, bf16[2,72,7168]{2,1,0:T(8,128)(2,1)} %bitcast.118), custom_call_target="tpu_custom_call" | custom-call | tf_op jit(solution)/shard_map/rows_to_experts/pallas_call | solution.py:206
  286.1 0.0 copy-start.3
  286.1 0.0 copy-start.6
  286.2 0.0 slice-start
  286.2 6.8 %fusion.27 = f32[576,256]{1,0:T(8,128)S(1)} fusion(bf16[576,7168]{1,0:T(8,128)(2,1)} %bitcast.114, bf16[1,7168,256]{2,1,0:T(8,128)(2,1)} %param.19), kind=kOutput, calls=%fused_computation.39 | convolution fusion | flops 2113929216 | bytes 12517376 | tf_op jit(solution)/shard_map/dot_general | solution.py:55
  293.0 0.0 slice-start.1
  293.0 0.0 copy-done.3
  293.0 0.9 copy-done.6
  293.9 0.0 copy-start.5
  293.9 3.1 fusion.29
  297.0 0.0 slice-done
  297.0 0.0 slice-done.1
  297.0 0.7 copy-done.5
  297.8 2.3 fusion.17
  300.1 17.8 %convolution_convert_fusion = bf16[576,7168]{1,0:T(8,128)(2,1)} fusion(bf16[1,256,7168]{2,1,0:T(8,128)(2,1)} %param.21, bf16[576,7168]{1,0:T(8,128)(2,1)} %bitcast.116, bf16[1,7168,256]{2,1,0:T(8,128)(2,1)} %param.20, f32[576,256]{1,0:T(8,128)} %fusion.29), kind=kOutput, calls=%fused_computation.1 | convolution fusion | flops 4232871936 | bytes 24444928 | tf_op jit(solution)/shard_map/dot_general | solution.py:51
  317.9 19.8 %fusion.25 = f32[576,7168]{1,0:T(8,128)} fusion(bf16[1,7168,256]{2,1,0:T(8,128)(2,1)} %param.19, f32[576,256]{1,0:T(8,128)S(1)} %fusion.17, bf16[576,7168]{1,0:T(8,128)(2,1)} %bitcast.115, bf16[1,7168,256]{2,1,0:T(8,128)(2,1)} %param.20, f32[576,256]{1,0:T(8,128)S(1)} %fusion.27), kind=kOutput, calls=%fused_computation.37 | convolution fusion | flops 4229332992 | bytes 33292288 | tf_op jit(solution)/shard_map/dot_general | solution.py:64
  337.7 12.6 %add_convert_fusion = bf16[576,7168]{1,0:T(8,128)(2,1)} fusion(f32[576,7168]{1,0:T(8,128)} %fusion.25, bf16[1,7168,256]{2,1,0:T(8,128)(2,1)} %param.20, f32[576,256]{1,0:T(8,128)S(1)} %fusion.17, f32[576,256]{1,0:T(8,128)S(1)} %fusion.27), kind=kOutput, calls=%fused_computation | convolution fusion | flops 2123071488 | bytes 29622272 | tf_op jit(solution)/shard_map/dot_general | solution.py:65
  350.3 198.0 %sums_to_tokens.1 = (bf16[2,72,7168]{2,1,0:T(8,128)(2,1)}, bf16[2,72,7168]{2,1,0:T(8,128)(2,1)}) custom-call(bf16[2,4,72,7168]{3,2,1,0:T(8,128)(2,1)} %bitcast.113, bf16[2,4,72,7168]{3,2,1,0:T(8,128)(2,1)} %bitcast.112), custom_call_target="tpu_custom_call" | custom-call | tf_op jit(solution)/shard_map/sums_to_tokens/pallas_call | solution.py:334
  548.2 0.0 copy-start.4
  548.3 2.6 fusion.9
  550.9 0.0 copy-done.4
  550.9 0.0 copy-start.2
  550.9 0.0 copy-start.7
  551.0 0.0 copy-start.11
  551.0 1.1 fusion.31
  552.0 0.1 collective-permute-start.1
  552.1 0.3 copy-done.2
  552.4 0.6 copy-done.7
  553.1 0.0 copy-done.11
  553.1 0.8 fusion.3
  553.9 0.1 collective-permute-start
  553.9 35.7 %collective-permute-done.1 = bf16[1,128,7168]{2,1,0:T(8,128)(2,1)S(1)} collective-permute-done((bf16[1,128,7168]{2,1,0:T(8,128)(2,1)S(1)}, bf16[1,128,7168]{2,1,0:T(8,128)(2,1)S(1)}, u32[]{:S(2)}, u32[]{:S(2)}) %collective-permute-start.1) | collective-permute-done | bytes 1835040 | tf_op jit(solution)/shard_map/ppermute | solution.py:19
  589.6 4.9 collective-permute-done
  594.5 1.2 copy.15
  595.8 1.2 copy.16
  (6 shorter events, 0.0 us)
Async XLA Ops:
  0.6 8.8 %copy-start = (bf16[1,128,7168]{2,1,0:T(8,128)(2,1)S(1)}, bf16[1,128,7168]{2,1,0:T(8,128)(2,1)}, u32[]{:S(2)}) copy-start(bf16[1,128,7168]{2,1,0:T(8,128)(2,1)} %param.14) | copy-start | bytes 5505028
  0.6 4.1 copy-start.9
  0.7 4.5 copy-start.10
  0.7 5.0 copy-start.12
  0.7 8.8 %copy-start.8 = (f32[1,7168]{1,0:T(1,128)S(1)}, f32[1,7168]{1,0:T(1,128)}, u32[]{:S(2)}) copy-start(f32[1,7168]{1,0:T(1,128)} %param.18) | copy-start | bytes 86020
  5.8 5.8 copy-start.1
  286.1 6.9 %copy-start.3 = (bf16[2,4,72,7168]{3,2,1,0:T(8,128)(2,1)S(1)}, bf16[2,4,72,7168]{3,2,1,0:T(8,128)(2,1)}, u32[]{:S(2)}) copy-start(bf16[2,4,72,7168]{3,2,1,0:T(8,128)(2,1)} %get-tuple-element.7) | copy-start | bytes 24772612
  286.1 7.8 %copy-start.6 = (bf16[1,7168,256]{2,1,0:T(8,128)(2,1)S(1)}, bf16[1,7168,256]{2,1,0:T(8,128)(2,1)}, u32[]{:S(2)}) copy-start(bf16[1,7168,256]{2,1,0:T(8,128)(2,1)} %param.19) | copy-start | bytes 11010052
  286.2 10.9 %slice-start = ((s8[8257536]{0:T(1024)(128)(4,1)}), s8[4194304]{0:T(1024)(128)(4,1)S(1)}, s32[]{:S(2)}) async-start(s8[8257536]{0:T(1024)(128)(4,1)} %bitcast.132), calls=%async_computation | async-start | bytes 8388608
  293.0 4.0 slice-start.1
  293.9 3.9 copy-start.5
  548.2 2.7 copy-start.4
  550.9 1.5 copy-start.2
  550.9 2.1 copy-start.7
  551.0 2.1 copy-start.11
  552.0 37.6 %collective-permute-start.1 = (bf16[1,128,7168]{2,1,0:T(8,128)(2,1)S(1)}, bf16[1,128,7168]{2,1,0:T(8,128)(2,1)S(1)}, u32[]{:S(2)}, u32[]{:S(2)}) collective-permute-start(bf16[1,128,7168]{2,1,0:T(8,128)(2,1)S(1)} %fusion.31), channel_id=1, source_target_pairs={{0,24},{8,0},{16,8},{24,16},{1,25},{9,1},{17,9},{25,17},{2,26},{10... | collective-permute-start | bytes 5505032 | tf_op jit(solution)/shard_map/ppermute | solution.py:19
  553.9 40.7 %collective-permute-start = (bf16[1,128,7168]{2,1,0:T(8,128)(2,1)S(1)}, bf16[1,128,7168]{2,1,0:T(8,128)(2,1)S(1)}, u32[]{:S(2)}, u32[]{:S(2)}) collective-permute-start(bf16[1,128,7168]{2,1,0:T(8,128)(2,1)S(1)} %fusion.3), channel_id=1, source_target_pairs={{0,8},{8,16},{16,24},{24,0},{1,9},{9,17},{17,25},{25,1},{2,10},{10... | collective-permute-start | bytes 5505032 | tf_op jit(solution)/shard_map/ppermute | solution.py:19

commit v3 on v2

v3 whole, which is shorter than its diff:
```python
import functools

import jax
import jax.numpy as jnp
from jax import lax
from jax.experimental import pallas as pl
from jax.experimental.pallas import tpu as pltpu
from jax.sharding import PartitionSpec as P

SHARDS = 4
TOP = 1


EPS = 1e-06


def normed(token_rows, gain_row):
    values = token_rows.astype(jnp.float32)
    factor = lax.rsqrt(jnp.mean(values * values, axis=-1, keepdims=True) + EPS)
    return values * factor * gain_row


def slot_tables(route_ids, gate_vals, experts_n, capacity):
    tok_rows, top_n = route_ids.shape
    flat_ids = route_ids.reshape(-1)
    one_hot = (flat_ids[:, None] == jnp.arange(experts_n, dtype=jnp.int32)[None, :]).astype(
        jnp.int32
    )
    slot_ids = jnp.sum((jnp.cumsum(one_hot, axis=0) - one_hot) * one_hot, axis=1)
    position = flat_ids * capacity + slot_ids
    places = jnp.arange(experts_n * capacity, dtype=jnp.int32)
    hit = position[None, :] == places[:, None]
    slot_gate = jnp.sum(jnp.where(hit, gate_vals.reshape(-1)[None, :], jnp.float32(0.0)), axis=1)
    select = jnp.sum(hit.reshape(-1, tok_rows, top_n), axis=2).astype(jnp.bfloat16)
    return select, slot_gate


def pick(select, rows):
    return jnp.dot(select, rows, preferred_element_type=jnp.float32)


def expert_forward(token_rows, gate_cols, up_cols, down_rows):
    pre_gate = jnp.dot(token_rows, gate_cols, preferred_element_type=jnp.float32)
    pre_up = jnp.dot(token_rows, up_cols, preferred_element_type=jnp.float32)
    hidden = (pre_gate * jax.nn.sigmoid(pre_gate) * pre_up).astype(jnp.bfloat16)
    return jnp.dot(hidden, down_rows, preferred_element_type=jnp.float32)


def expert_backward(token_rows, upstream, gate_cols, up_cols, down_rows):
    pre_gate = jnp.dot(token_rows, gate_cols, preferred_element_type=jnp.float32)
    pre_up = jnp.dot(token_rows, up_cols, preferred_element_type=jnp.float32)
    contract = (((1,), (1,)), ((), ()))
    grad_hidden = lax.dot_general(upstream, down_rows, contract, preferred_element_type=jnp.float32)
    sigmoid_gate = jax.nn.sigmoid(pre_gate)
    grad_gate = (
        grad_hidden * pre_up * sigmoid_gate * (1.0 + pre_gate * (1.0 - sigmoid_gate))
    ).astype(jnp.bfloat16)
    grad_up = (grad_hidden * pre_gate * sigmoid_gate).astype(jnp.bfloat16)
    first = lax.dot_general(grad_gate, gate_cols, contract, preferred_element_type=jnp.float32)
    second = lax.dot_general(grad_up, up_cols, contract, preferred_element_type=jnp.float32)
    return first + second


MESH = pl.DeviceIdType.MESH
VMEM_BYTES = 58 * 1024 * 1024


def places(experts_n):
    me = lax.axis_index("expert")
    group, shard = me // SHARDS, me % SHARDS
    near = shard + 1 - 2 * (shard % 2)
    mirrored, shifted = SHARDS - 1 - shard, (shard + 2) % SHARDS
    if experts_n == 2:
        return group, shard, (near, shifted), mirrored
    return group, shard, (near, mirrored), shifted


def pieces(features, experts_n):
    first = features // 4 * 3 if experts_n == 2 else features // 2
    return pl.ds(0, first), pl.ds(first, features - first)


def section_at(by):
    sections = lax.axis_size("section")
    return (lax.axis_index("section") + by + sections) % sections


def greet(partners):
    barrier = pltpu.get_barrier_semaphore()
    for section, expert in partners:
        pl.semaphore_signal(
            barrier, inc=1, device_id={"section": section, "expert": expert}, device_id_type=MESH
        )
    pl.semaphore_wait(barrier, len(partners))


def remote(src, dst, send, recv, target, by=0):
    return pltpu.make_async_remote_copy(
        src_ref=src,
        dst_ref=dst,
        send_sem=send,
        recv_sem=recv,
        device_id={"section": section_at(by), "expert": target},
        device_id_type=MESH,
    )


def outward_kernel(experts_n, arrays, shifts, *refs):
    extras = len(shifts)
    inputs, outputs = refs[: arrays + extras], refs[arrays + extras : 2 * (arrays + extras)]
    packed, passed = inputs[:arrays], inputs[arrays:]
    gathered, arrived = outputs[:arrays], outputs[arrays:]
    (
        cross_send,
        cross_recv,
        ring_send,
        ring_recv,
        part_send,
        part_recv,
        local_sem,
        pass_send,
        pass_recv,
    ) = refs[2 * (arrays + extras) :]
    group, shard, links, far = places(experts_n)
    me = lax.axis_index("expert")
    here = section_at(0)
    greet(
        [(here, group * SHARDS + link) for link in links]
        + [(here, (group + step) % experts_n * SHARDS + shard) for step in range(1, experts_n)]
        + [(section_at(by), me) for by in (1, -1)]
    )
    cols = pieces(packed[0].shape[2], experts_n)
    started = []

    def begin(copy):
        copy.start()
        started.append(copy)
        return copy

    crossing, ring, parts, local = {}, {}, {}, []
    for a in range(arrays):
        for step in range(1, experts_n):
            expert = (group + step) % experts_n
            crossing[a, step] = begin(
                remote(
                    packed[a].at[expert],
                    gathered[a].at[group, shard],
                    cross_send.at[a, step],
                    cross_recv.at[a, step],
                    expert * SHARDS + shard,
                )
            )
        for side, target in enumerate(links):
            ring[a, 0, side] = begin(
                remote(
                    packed[a].at[group],
                    gathered[a].at[group, shard],
                    ring_send.at[a, 0, side],
                    ring_recv.at[a, 0, side],
                    group * SHARDS + target,
                )
            )
        copy = pltpu.make_async_copy(
            packed[a].at[group], gathered[a].at[group, shard], local_sem.at[a]
        )
        copy.start()
        local.append(copy)
    passing = [
        begin(remote(passed[i], arrived[i], pass_send.at[i], pass_recv.at[i], me, by))
        for i, by in enumerate(shifts)
    ]

    def relay(a, step):
        origin = (group + experts_n - step) % experts_n
        for side, target in enumerate(links):
            ring[a, step, 1 - side].wait_recv()
            block = gathered[a].at[origin, links[1 - side], :, cols[side]]
            parts[a, step, side] = begin(
                remote(
                    block,
                    block,
                    part_send.at[a, step, side],
                    part_recv.at[a, step, side],
                    group * SHARDS + target,
                )
            )

    for a in range(arrays):
        for step in range(1, experts_n):
            origin = (group + experts_n - step) % experts_n
            crossing[a, step].wait_recv()
            block = gathered[a].at[origin, shard]
            for side, target in enumerate(links):
                ring[a, step, side] = begin(
                    remote(
                        block,
                        block,
                        ring_send.at[a, step, side],
                        ring_recv.at[a, step, side],
                        group * SHARDS + target,
                    )
                )
        relay(a, 0)
        if a > 0:
            for step in range(1, experts_n):
                relay(a - 1, step)
    for step in range(1, experts_n):
        relay(arrays - 1, step)
    for copy in list(parts.values()) + passing:
        copy.wait_recv()
    for copy in local:
        copy.wait()
    for copy in started:
        copy.wait_send()


def outward_call(packed, passed, shifts):
    arrays, extras = len(packed), len(passed)
    experts_n, capacity, features = packed[0].shape
    dma = pltpu.SemaphoreType.DMA
    shape = jax.ShapeDtypeStruct((experts_n, SHARDS, capacity, features), jnp.bfloat16)
    outs = pl.pallas_call(
        functools.partial(outward_kernel, experts_n, arrays, shifts),
        out_shape=[shape] * arrays + [jax.ShapeDtypeStruct(v.shape, v.dtype) for v in passed],
        in_specs=[pl.BlockSpec(memory_space=pl.ANY)] * (arrays + extras),
        out_specs=[pl.BlockSpec(memory_space=pl.ANY)] * (arrays + extras),
        scratch_shapes=[
            dma((arrays, experts_n)),
            dma((arrays, experts_n)),
            dma((arrays, experts_n, 2)),
            dma((arrays, experts_n, 2)),
            dma((arrays, experts_n, 2)),
            dma((arrays, experts_n, 2)),
            dma((arrays,)),
            dma((extras,)),
            dma((extras,)),
        ],
        compiler_params=pltpu.CompilerParams(
            collective_id=0, has_side_effects=True, vmem_limit_bytes=VMEM_BYTES
        ),
        name="rows_to_experts",
    )(*packed, *passed)
    return outs[:arrays], outs[arrays:]


def add_into(dst, terms, columns):
    tile = 512 if columns % 512 == 0 else 256 if columns % 256 == 0 else 128

    @pl.loop(0, columns // tile)
    def _(i):
        at = pl.ds(pl.multiple_of(i * tile, tile), tile)
        total = terms[0][:, at].astype(jnp.float32)
        for term in terms[1:]:
            total = total + term[:, at].astype(jnp.float32)
        dst[:, at] = total.astype(dst.dtype)


def return_kernel(experts_n, shifts, *refs):
    arrays = len(shifts)
    partial, summed = refs[:arrays], refs[arrays : 2 * arrays]
    (
        far_first,
        far_second,
        near_in,
        total,
        far_send,
        far_recv,
        near_send,
        near_recv,
        out_send,
        out_recv,
    ) = refs[2 * arrays :]
    far_in = (far_first, far_second)
    group, shard, links, far = places(experts_n)
    here = section_at(0)
    greet(
        [(here, group * SHARDS + link) for link in links]
        + [
            (section_at(by), expert * SHARDS + shard)
            for by in (1, -1)
            for expert in range(experts_n)
        ]
    )
    features = partial[0].shape[3]
    cols = pieces(features, experts_n)
    started, far_copies, near_copies, out_copies = [], {}, {}, {}

    def begin(copy):
        copy.start()
        started.append(copy)
        return copy

    order = [(a, step) for a in range(arrays) for step in list(range(1, experts_n)) + [0]]
    for a, step in order:
        origin = (group + step) % experts_n
        for side, target in enumerate(links):
            far_copies[a, step, side] = begin(
                remote(
                    partial[a].at[origin, far, :, cols[side]],
                    far_in[side].at[a, step],
                    far_send.at[a, step, side],
                    far_recv.at[a, step, side],
                    group * SHARDS + target,
                )
            )
    for a, step in order:
        origin = (group + step) % experts_n
        for side, target in enumerate(links):
            near_copies[a, step, side, 1] = begin(
                remote(
                    partial[a].at[origin, target, :, cols[side]],
                    near_in.at[a, step, side, :, cols[side]],
                    near_send.at[a, step, side, 1],
                    near_recv.at[a, step, side, 1],
                    group * SHARDS + target,
                )
            )
    for a, step in order:
        origin = (group + step) % experts_n
        for side in range(2):
            target = links[1 - side]
            far_copies[a, step, side].wait_recv()
            block = far_in[side].at[a, step]
            add_into(block, (block, partial[a].at[origin, target, :, cols[side]]), cols[side].size)
            near_copies[a, step, 1 - side, 0] = begin(
                remote(
                    block,
                    near_in.at[a, step, 1 - side, :, cols[side]],
                    near_send.at[a, step, 1 - side, 0],
                    near_recv.at[a, step, 1 - side, 0],
                    group * SHARDS + target,
                )
            )
    for a, step in order:
        origin = (group + step) % experts_n
        for side in range(2):
            for part in range(2):
                near_copies[a, step, side, part].wait_recv()
        result = total.at[a, step]
        add_into(
            result,
            (near_in.at[a, step, 0], near_in.at[a, step, 1], partial[a].at[origin, shard]),
            features,
        )
        out_copies[a, step] = begin(
            remote(
                result,
                summed[a].at[group],
                out_send.at[a, step],
                out_recv.at[a, step],
                origin * SHARDS + shard,
                shifts[a],
            )
        )
    for copy in out_copies.values():
        copy.wait_recv()
    for copy in started:
        copy.wait_send()


def return_call(partial, shifts):
    arrays = len(partial)
    experts_n, unused, capacity, features = partial[0].shape
    dma = pltpu.SemaphoreType.DMA
    shape = jax.ShapeDtypeStruct((experts_n, capacity, features), jnp.bfloat16)
    first, second = pieces(features, experts_n)
    return pl.pallas_call(
        functools.partial(return_kernel, experts_n, shifts),
        out_shape=[shape] * arrays,
        in_specs=[pl.BlockSpec(memory_space=pltpu.VMEM)] * arrays,
        out_specs=[pl.BlockSpec(memory_space=pl.ANY)] * arrays,
        scratch_shapes=[
            pltpu.VMEM((arrays, experts_n, capacity, first.size), jnp.bfloat16),
            pltpu.VMEM((arrays, experts_n, capacity, second.size), jnp.bfloat16),
            pltpu.VMEM((arrays, experts_n, 2, capacity, features), jnp.bfloat16),
            pltpu.VMEM((arrays, experts_n, capacity, features), jnp.bfloat16),
            dma((arrays, experts_n, 2)),
            dma((arrays, experts_n, 2)),
            dma((arrays, experts_n, 2, 2)),
            dma((arrays, experts_n, 2, 2)),
            dma((arrays, experts_n)),
            dma((arrays, experts_n)),
        ],
        compiler_params=pltpu.CompilerParams(
            collective_id=1, has_side_effects=True, vmem_limit_bytes=VMEM_BYTES
        ),
        name="sums_to_tokens",
    )(*partial)


def local(
    acts_fwd,
    routes_fwd,
    gates_fwd,
    stash_bwd,
    grads_bwd,
    routes_bwd,
    gates_bwd,
    gain,
    w_gate,
    w_up,
    w_down,
):
    devices = lax.axis_size("expert")
    experts_n = devices // SHARDS
    tok_rows, features = acts_fwd.shape[1:]
    capacity = min(tok_rows, 9 * tok_rows * TOP // (8 * experts_n))
    gate_cols = w_gate[0]
    up_cols = w_up[0]
    down_rows = w_down[0]
    gain_row = gain[0]
    entering = acts_fwd[0]
    select_fwd, unused_gate = slot_tables(routes_fwd[0], gates_fwd[0], experts_n, capacity)
    rows_fwd = pick(select_fwd, normed(entering, gain_row).astype(jnp.bfloat16)).astype(jnp.bfloat16)
    stashed = stash_bwd[0]
    upstream = grads_bwd[0]
    select_bwd, slot_gate = slot_tables(routes_bwd[0], gates_bwd[0], experts_n, capacity)
    rows_bwd = pick(select_bwd, normed(stashed, gain_row).astype(jnp.bfloat16)).astype(jnp.bfloat16)
    rows_grad = (pick(select_bwd, upstream) * slot_gate[:, None]).astype(jnp.bfloat16)
    packed = [
        rows.reshape(experts_n, capacity, features) for rows in (rows_fwd, rows_bwd, rows_grad)
    ]
    wide = -(-experts_n * capacity // 128) * 128

    def token_table(select):
        return jnp.pad(select.T, ((0, 0), (0, wide - experts_n * capacity)))

    passed = (
        (acts_fwd, 1),
        (token_table(select_fwd), 1),
        (jnp.broadcast_to(gates_fwd[0], (tok_rows, 128)), 1),
        (stash_bwd, -1),
        (grads_bwd, -1),
        (token_table(select_bwd), -1),
        (gain.reshape(features // 128, 128), -1),
    )
    gathered, arrived = outward_call(
        packed, [value for value, by in passed], tuple(by for value, by in passed)
    )
    all_fwd, all_bwd, all_grad = [rows.reshape(-1, features) for rows in gathered]
    results = (
        expert_forward(all_fwd, gate_cols, up_cols, down_rows),
        expert_backward(all_bwd, all_grad, gate_cols, up_cols, down_rows),
    )
    partial = [
        result.astype(jnp.bfloat16).reshape(experts_n, SHARDS, capacity, features)
        for result in results
    ]
    back_fwd, back_bwd = [rows.reshape(-1, features) for rows in return_call(partial, (1, -1))]
    acts, table_fwd, gates, stash, grads, table_bwd, gain_there = arrived
    filled = experts_n * capacity
    mixture = gates[:, :1] * pick(table_fwd[:, :filled], back_fwd)
    layer_out = (acts[0].astype(jnp.float32) + mixture).astype(jnp.bfloat16)
    grad_normed = pick(table_bwd[:, :filled], back_bwd)
    gain_row = gain_there.reshape(features)

    def norm_only(values):
        return normed(values, gain_row)

    unused, pullback = jax.vjp(norm_only, stash[0].astype(jnp.float32))
    grad_input = (grads[0].astype(jnp.float32) + pullback(grad_normed)[0]).astype(jnp.bfloat16)
    return (layer_out[None], grad_input[None])


def solution(mesh):
    return jax.shard_map(
        local,
        mesh=mesh,
        in_specs=(
            P("section", "expert", None),
            P("section", "expert", None),
            P("section", "expert", None),
            P("section", "expert", None),
            P("section", "expert", None),
            P("section", "expert", None),
            P("section", "expert", None),
            P("section", None),
            P("section", None, "expert"),
            P("section", None, "expert"),
            P("section", "expert", None),
        ),
        out_specs=(P("section", "expert", None), P("section", "expert", None)),
        check_vma=False,
    )
```

time: 597 us -> 578 us (0.968)
  waiting for transfers between devices: 40.6 us -> 0 us
  Pallas kernels: 470 us -> 491 us
    ppermute x2 -> x0, waiting for transfers between devices: 40.6 us -> none  [from_behind(): lax.ppermute(value, axis, [(i, (i + by) % devices) for i in range(devices)])]
    pallas_call x2, Pallas kernels: 470 us -> 491 us  [the longest x1 253 us: outward_call(): pl.pallas_call(functools.partial(outward_kernel, experts_n, arrays, shift...]
  transfers between devices with their start and end apart: 2 -> 0, of which waited for: 2 -> 0; matrix products, arithmetic and copies ran while one was open for 0% -> 0% of each run, Pallas kernels for 0% -> 0%
where the time goes in v3:
time: 578 us
  Pallas kernels  491 us (85%)
  matrix products  74.4 us (13%)
  other arithmetic  7.48 us (1%)
    pallas_call x1, Pallas kernels, outward_call(): pl.pallas_call(functools.partial(outward_kernel, experts_n, arrays, shift...  253 us
    pallas_call x1, Pallas kernels, return_call(): pl.pallas_call(functools.partial(return_kernel, experts_n, shifts), out_s...  238 us
    dot_general x1, matrix products, expert_backward(): lax.dot_general(grad_gate, gate_cols, contract, preferred_element_type=jn...  19.8 us
    dot_general x1, matrix products, expert_forward(): return jnp.dot(hidden, down_rows, preferred_element_type=jnp.float32)  17.6 us
    dot_general x5, matrix products, pick(): return jnp.dot(select, rows, preferred_element_type=jnp.float32)  12.9 us
    dot_general x1, matrix products, expert_backward(): lax.dot_general(grad_up, up_cols, contract, preferred_element_type=jnp.fl...  12.6 us

profile of v3, /device:TPU:0, one launch (start us, length us, event | category | flops | bytes accessed | tf_op | source)
XLA Modules:
  0.0 578.0 jit_solution(18295075111295270316)
XLA Ops:
  0.6 0.0 copy-start.13
  0.6 0.0 copy-start.12
  0.7 0.0 copy-start.15
  0.7 0.0 copy-start.14
  0.7 1.9 fusion.4
  2.6 0.0 copy-start.1
  2.6 0.0 copy-start.8
  2.6 2.1 fusion.7
  4.7 0.0 copy-done.14
  4.7 0.7 broadcast_in_dim.44.refs_5_
  5.4 0.0 copy-done.12
  5.5 0.1 fusion.74
  5.5 0.2 reduce_window_sum.17
  5.7 0.2 select_reduce_fusion.2
  5.9 0.1 convert_convert_fusion.1
  6.0 0.6 pad.7.refs_4_
  6.6 0.0 copy-done.13
  6.6 0.1 fusion.73
  6.7 0.2 reduce_window_sum.18
  6.9 0.2 select_reduce_fusion.1
  7.1 0.0 copy-done.15
  7.1 0.1 select_reduce_fusion
  7.2 0.1 convert_convert_fusion
  7.3 0.6 pad.8.refs_8_
  8.0 0.0 copy-start
  8.0 3.7 fusion.1
  11.7 0.0 copy-done.1
  11.7 0.0 copy-done.8
  11.7 2.1 convolution_convert_fusion.1
  13.7 0.0 copy-done
  13.7 2.2 convolution_convert_fusion.2
  15.9 252.6 %rows_to_experts.1 = (bf16[2,4,72,7168]{3,2,1,0:T(8,128)(2,1)}, bf16[2,4,72,7168]{3,2,1,0:T(8,128)(2,1)}, bf16[2,4,72,7168]{3,2,1,0:T(8,128)(2,1)}, bf16[1,128,7...) custom-call(bf16[2,72,7168]{2,1,0:T(8,128)(2,1)} %bitcast.102, ...), custom_call_target="tpu_custom_call" | custom-call | tf_op jit(solution)/shard_map/rows_to_experts/pallas_call | solution.py:222
  268.6 0.9 slice_reduce_fusion
  269.5 0.0 copy-start.2
  269.5 0.0 copy-start.4
  269.5 0.0 slice-start
  269.5 6.9 %fusion.14 = f32[576,256]{1,0:T(8,128)S(1)} fusion(bf16[576,7168]{1,0:T(8,128)(2,1)} %bitcast.115, bf16[1,256,7168]{2,1,0:T(8,128)(2,1)} %param.21), kind=kOutput, calls=%fused_computation.29 | convolution fusion | flops 2113929216 | bytes 12517376 | tf_op jit(solution)/shard_map/dot_general | solution.py:53
  276.4 0.0 copy-done.2
  276.4 0.9 copy-done.4
  277.3 0.0 slice-start.1
  277.3 2.3 fusion.24
  279.6 0.0 slice-done
  279.6 0.3 slice-done.1
  279.9 2.3 fusion.26
  282.2 17.6 %convolution_convert_fusion = bf16[576,7168]{1,0:T(8,128)(2,1)} fusion(bf16[1,256,7168]{2,1,0:T(8,128)(2,1)} %param.21, bf16[576,7168]{1,0:T(8,128)(2,1)} %bitcast.96, bf16[1,7168,256]{2,1,0:T(8,128)(2,1)} %param.20, f32[576,256]{1,0:T(8,128)S(1)} %fusion.26), kind=kOutput, calls=%fused_computation.1 | convolution fusion | flops 4232871936 | bytes 24444928 | tf_op jit(solution)/shard_map/dot_general | solution.py:46
  299.8 19.8 %fusion.22 = f32[576,7168]{1,0:T(8,128)} fusion(bf16[1,7168,256]{2,1,0:T(8,128)(2,1)} %param.19, f32[576,256]{1,0:T(8,128)S(1)} %fusion.14, bf16[576,7168]{1,0:T(8,128)(2,1)} %bitcast.94, bf16[1,7168,256]{2,1,0:T(8,128)(2,1)} %param.20, f32[576,256]{1,0:T(8,128)S(1)} %fusion.24), kind=kOutput, calls=%fused_computation.37 | convolution fusion | flops 4229332992 | bytes 33292288 | tf_op jit(solution)/shard_map/dot_general | solution.py:59
  319.6 12.6 %add_convert_fusion = bf16[576,7168]{1,0:T(8,128)(2,1)} fusion(f32[576,7168]{1,0:T(8,128)} %fusion.22, bf16[1,7168,256]{2,1,0:T(8,128)(2,1)} %param.20, f32[576,256]{1,0:T(8,128)S(1)} %fusion.14, f32[576,256]{1,0:T(8,128)S(1)} %fusion.24), kind=kOutput, calls=%fused_computation | convolution fusion | flops 2123071488 | bytes 29622272 | tf_op jit(solution)/shard_map/dot_general | solution.py:60
  332.2 0.0 copy-start.7
  332.2 238.3 %sums_to_tokens.1 = (bf16[2,72,7168]{2,1,0:T(8,128)(2,1)}, bf16[2,72,7168]{2,1,0:T(8,128)(2,1)}) custom-call(bf16[2,4,72,7168]{3,2,1,0:T(8,128)(2,1)} %bitcast.93, bf16[2,4,72,7168]{3,2,1,0:T(8,128)(2,1)} %bitcast.92), custom_call_target="tpu_custom_call" | custom-call | tf_op jit(solution)/shard_map/sums_to_tokens/pallas_call | solution.py:367
  570.5 0.0 copy-start.3
  570.5 0.0 copy-start.5
  570.5 0.0 copy-start.9
  570.5 0.0 copy-start.11
  570.5 0.0 copy-done.7
  570.6 0.0 copy-done.10
  570.6 3.6 fusion.3
  574.2 0.0 copy-done.3
  574.2 0.0 copy-done.5
  574.2 0.0 copy-done.9
  574.2 0.0 copy-done.11
  574.2 0.0 copy-start.6
  574.2 1.3 fusion.12
  575.6 0.2 copy-done.6
  575.7 2.3 fusion.28
  (7 shorter events, 0.0 us)
Async XLA Ops:
  0.6 6.0 %copy-start.13 = (s32[1,128,1]{1,2,0:T(1,128)S(1)}, s32[1,128,1]{1,2,0:T(1,128)}, u32[]{:S(2)}) copy-start(s32[1,128,1]{1,2,0:T(1,128)} %param.16) | copy-start | bytes 1540
  0.6 4.8 copy-start.12
  0.7 6.4 %copy-start.15 = (f32[1,128,1]{1,2,0:T(1,128)S(1)}, f32[1,128,1]{1,2,0:T(1,128)}, u32[]{:S(2)}) copy-start(f32[1,128,1]{1,2,0:T(1,128)} %param.17) | copy-start | bytes 1540
  0.7 4.1 copy-start.14
  2.6 9.1 %copy-start.1 = (bf16[1,128,7168]{2,1,0:T(8,128)(2,1)S(1)}, bf16[1,128,7168]{2,1,0:T(8,128)(2,1)}, u32[]{:S(2)}) copy-start(bf16[1,128,7168]{2,1,0:T(8,128)(2,1)} %refs_6_.1) | copy-start | bytes 5505028
  2.6 9.0 %copy-start.8 = (f32[1,7168]{1,0:T(1,128)S(1)}, f32[1,7168]{1,0:T(1,128)}, u32[]{:S(2)}) copy-start(f32[1,7168]{1,0:T(1,128)} %param.18) | copy-start | bytes 86020
  8.0 5.8 %copy-start = (bf16[1,128,7168]{2,1,0:T(8,128)(2,1)S(1)}, bf16[1,128,7168]{2,1,0:T(8,128)(2,1)}, u32[]{:S(2)}) copy-start(bf16[1,128,7168]{2,1,0:T(8,128)(2,1)} %refs_3_.1) | copy-start | bytes 5505028
  269.5 6.9 %copy-start.2 = (bf16[2,4,72,7168]{3,2,1,0:T(8,128)(2,1)S(1)}, bf16[2,4,72,7168]{3,2,1,0:T(8,128)(2,1)}, u32[]{:S(2)}) copy-start(bf16[2,4,72,7168]{3,2,1,0:T(8,128)(2,1)} %get-tuple-element.19) | copy-start | bytes 24772612
  269.5 7.8 %copy-start.4 = (bf16[1,7168,256]{2,1,0:T(8,128)(2,1)S(1)}, bf16[1,7168,256]{2,1,0:T(8,128)(2,1)}, u32[]{:S(2)}) copy-start(bf16[1,7168,256]{2,1,0:T(8,128)(2,1)} %param.19) | copy-start | bytes 11010052
  269.5 10.1 %slice-start = ((s8[8257536]{0:T(1024)(128)(4,1)}), s8[4194304]{0:T(1024)(128)(4,1)S(1)}, s32[]{:S(2)}) async-start(s8[8257536]{0:T(1024)(128)(4,1)} %bitcast.97), calls=%async_computation | async-start | bytes 8388608
  277.3 2.6 slice-start.1
  332.2 238.3 %copy-start.7 = (bf16[1,128,7168]{2,1,0:T(8,128)(2,1)S(1)}, bf16[1,128,7168]{2,1,0:T(8,128)(2,1)}, u32[]{:S(2)}) copy-start(bf16[1,128,7168]{2,1,0:T(8,128)(2,1)} %get-tuple-element.14) | copy-start | bytes 5505028
  332.2 238.4 %copy-start.10 = (bf16[128,256]{1,0:T(8,128)(2,1)S(1)}, bf16[128,256]{1,0:T(8,128)(2,1)}, u32[]{:S(2)}) copy-start(bf16[128,256]{1,0:T(8,128)(2,1)} %get-tuple-element.16) | copy-start | bytes 196612
  570.5 3.7 copy-start.3
  570.5 3.7 copy-start.5
  570.5 3.7 copy-start.9
  570.5 3.7 copy-start.11
  574.2 1.5 copy-start.6

commit v4 on v3

--- a/solution.py
+++ b/solution.py
@@ -63,6 +63,8 @@
 
 MESH = pl.DeviceIdType.MESH
 VMEM_BYTES = 58 * 1024 * 1024
+CHUNKS = 2
+WINDOW = 2
 
 
 def places(experts_n):
@@ -75,9 +77,9 @@
     return group, shard, (near, mirrored), shifted
 
 
-def pieces(features, experts_n):
+def pieces(features, experts_n, start=0):
     first = features // 4 * 3 if experts_n == 2 else features // 2
-    return pl.ds(0, first), pl.ds(first, features - first)
+    return pl.ds(start, first), pl.ds(start + first, features - first)
 
 
 def section_at(by):
@@ -281,8 +283,7 @@
             for expert in range(experts_n)
         ]
     )
-    features = partial[0].shape[3]
-    cols = pieces(features, experts_n)
+    width = partial[0].shape[3] // CHUNKS
     started, far_copies, near_copies, out_copies = [], {}, {}, {}
 
     def begin(copy):
@@ -290,68 +291,94 @@
         started.append(copy)
         return copy
 
-    order = [(a, step) for a in range(arrays) for step in list(range(1, experts_n)) + [0]]
-    for a, step in order:
+    order = [
+        (a, step, c)
+        for step in list(range(1, experts_n)) + [0]
+        for a in range(arrays)
+        for c in range(CHUNKS)
+    ]
+
+    def columns(c):
+        return pieces(width, experts_n, c * width)
+
+    def send(a, step, c):
         origin = (group + step) % experts_n
+        cols = columns(c)
         for side, target in enumerate(links):
-            far_copies[a, step, side] = begin(
+            far_copies[a, step, c, side] = begin(
                 remote(
                     partial[a].at[origin, far, :, cols[side]],
-                    far_in[side].at[a, step],
-                    far_send.at[a, step, side],
-                    far_recv.at[a, step, side],
+                    far_in[side].at[a, step, c],
+                    far_send.at[a, step, c, side],
+                    far_recv.at[a, step, c, side],
                     group * SHARDS + target,
                 )
             )
-    for a, step in order:
-        origin = (group + step) % experts_n
         for side, target in enumerate(links):
-            near_copies[a, step, side, 1] = begin(
+            near_copies[a, step, c, side, 1] = begin(
                 remote(
                     partial[a].at[origin, target, :, cols[side]],
                     near_in.at[a, step, side, :, cols[side]],
-                    near_send.at[a, step, side, 1],
-                    near_recv.at[a, step, side, 1],
+                    near_send.at[a, step, c, side, 1],
+                    near_recv.at[a, step, c, side, 1],
                     group * SHARDS + target,
                 )
             )
-    for a, step in order:
+
+    def merge(a, step, c):
         origin = (group + step) % experts_n
+        cols = columns(c)
         for side in range(2):
             target = links[1 - side]
-            far_copies[a, step, side].wait_recv()
-            block = far_in[side].at[a, step]
+            far_copies[a, step, c, side].wait_recv()
+            block = far_in[side].at[a, step, c]
             add_into(block, (block, partial[a].at[origin, target, :, cols[side]]), cols[side].size)
-            near_copies[a, step, 1 - side, 0] = begin(
+            near_copies[a, step, c, 1 - side, 0] = begin(
                 remote(
                     block,
                     near_in.at[a, step, 1 - side, :, cols[side]],
-                    near_send.at[a, step, 1 - side, 0],
-                    near_recv.at[a, step, 1 - side, 0],
+                    near_send.at[a, step, c, 1 - side, 0],
+                    near_recv.at[a, step, c, 1 - side, 0],
                     group * SHARDS + target,
                 )
             )
-    for a, step in order:
+
+    def finish(a, step, c):
         origin = (group + step) % experts_n
+        whole = pl.ds(c * width, width)
         for side in range(2):
             for part in range(2):
-                near_copies[a, step, side, part].wait_recv()
-        result = total.at[a, step]
+                near_copies[a, step, c, side, part].wait_recv()
+        result = total.at[a, step, :, whole]
         add_into(
             result,
-            (near_in.at[a, step, 0], near_in.at[a, step, 1], partial[a].at[origin, shard]),
-            features,
+            (
+                near_in.at[a, step, 0, :, whole],
+                near_in.at[a, step, 1, :, whole],
+                partial[a].at[origin, shard, :, whole],
+            ),
+            width,
         )
-        out_copies[a, step] = begin(
+        out_copies[a, step, c] = begin(
             remote(
                 result,
-                summed[a].at[group],
-                out_send.at[a, step],
-                out_recv.at[a, step],
+                summed[a].at[group, :, whole],
+                out_send.at[a, step, c],
+                out_recv.at[a, step, c],
                 origin * SHARDS + shard,
                 shifts[a],
             )
         )
+
+    for item in order[:WINDOW]:
+        send(*item)
+    for i, item in enumerate(order):
+        merge(*item)
+        if i + WINDOW < len(order):
+            send(*order[i + WINDOW])
+        if i > 0:
+            finish(*order[i - 1])
+    finish(*order[-1])
     for copy in out_copies.values():
         copy.wait_recv()
     for copy in started:
@@ -363,23 +390,23 @@
     experts_n, unused, capacity, features = partial[0].shape
     dma = pltpu.SemaphoreType.DMA
     shape = jax.ShapeDtypeStruct((experts_n, capacity, features), jnp.bfloat16)
-    first, second = pieces(features, experts_n)
+    first, second = pieces(features // CHUNKS, experts_n)
     return pl.pallas_call(
         functools.partial(return_kernel, experts_n, shifts),
         out_shape=[shape] * arrays,
         in_specs=[pl.BlockSpec(memory_space=pltpu.VMEM)] * arrays,
         out_specs=[pl.BlockSpec(memory_space=pl.ANY)] * arrays,
         scratch_shapes=[
-            pltpu.VMEM((arrays, experts_n, capacity, first.size), jnp.bfloat16),
-            pltpu.VMEM((arrays, experts_n, capacity, second.size), jnp.bfloat16),
+            pltpu.VMEM((arrays, experts_n, CHUNKS, capacity, first.size), jnp.bfloat16),
+            pltpu.VMEM((arrays, experts_n, CHUNKS, capacity, second.size), jnp.bfloat16),
             pltpu.VMEM((arrays, experts_n, 2, capacity, features), jnp.bfloat16),
             pltpu.VMEM((arrays, experts_n, capacity, features), jnp.bfloat16),
-            dma((arrays, experts_n, 2)),
-            dma((arrays, experts_n, 2)),
-            dma((arrays, experts_n, 2, 2)),
-            dma((arrays, experts_n, 2, 2)),
-            dma((arrays, experts_n)),
-            dma((arrays, experts_n)),
+            dma((arrays, experts_n, CHUNKS, 2)),
+            dma((arrays, experts_n, CHUNKS, 2)),
+            dma((arrays, experts_n, CHUNKS, 2, 2)),
+            dma((arrays, experts_n, CHUNKS, 2, 2)),
+            dma((arrays, experts_n, CHUNKS)),
+            dma((arrays, experts_n, CHUNKS)),
         ],
         compiler_params=pltpu.CompilerParams(
             collective_id=1, has_side_effects=True, vmem_limit_bytes=VMEM_BYTES

time: 578 us -> 519 us (0.90)
  Pallas kernels: 491 us -> 430 us
    pallas_call x1, Pallas kernels: 238 us -> 177 us  [return_call(): pl.pallas_call(functools.partial(return_kernel, experts_n, shifts), out_s...]
where the time goes in v4:
time: 519 us; the launch traced here: 517 us
  Pallas kernels  430 us (83%)
  matrix products  74.4 us (14%)
  other arithmetic  7.48 us (1%)
    pallas_call x1, Pallas kernels, outward_call(): pl.pallas_call(functools.partial(outward_kernel, experts_n, arrays, shift...  253 us
    pallas_call x1, Pallas kernels, return_call(): pl.pallas_call(functools.partial(return_kernel, experts_n, shifts), out_s...  177 us
    dot_general x1, matrix products, expert_backward(): lax.dot_general(grad_gate, gate_cols, contract, preferred_element_type=jn...  19.8 us
    dot_general x1, matrix products, expert_forward(): return jnp.dot(hidden, down_rows, preferred_element_type=jnp.float32)  17.6 us
    dot_general x5, matrix products, pick(): return jnp.dot(select, rows, preferred_element_type=jnp.float32)  12.9 us
    dot_general x1, matrix products, expert_backward(): lax.dot_general(grad_up, up_cols, contract, preferred_element_type=jnp.fl...  12.6 us

profile of v4, /device:TPU:0, one launch (start us, length us, event | category | flops | bytes accessed | tf_op | source)
XLA Modules:
  0.0 517.0 jit_solution(2231290393249137321)
XLA Ops:
  0.6 0.0 copy-start.13
  0.6 0.0 copy-start.12
  0.7 0.0 copy-start.15
  0.7 0.0 copy-start.14
  0.7 1.9 fusion.4
  2.6 0.0 copy-start.1
  2.6 0.0 copy-start.8
  2.6 2.1 fusion.7
  4.7 0.0 copy-done.14
  4.7 0.7 broadcast_in_dim.44.refs_5_
  5.4 0.0 copy-done.12
  5.5 0.1 fusion.74
  5.5 0.2 reduce_window_sum.17
  5.7 0.2 select_reduce_fusion.2
  5.9 0.1 convert_convert_fusion.1
  6.0 0.6 pad.7.refs_4_
  6.6 0.0 copy-done.13
  6.6 0.1 fusion.73
  6.7 0.2 reduce_window_sum.18
  6.9 0.2 select_reduce_fusion.1
  7.1 0.0 copy-done.15
  7.1 0.1 select_reduce_fusion
  7.2 0.1 convert_convert_fusion
  7.3 0.6 pad.8.refs_8_
  8.0 0.0 copy-start
  8.0 3.7 fusion.1
  11.7 0.0 copy-done.1
  11.7 0.0 copy-done.8
  11.7 2.1 convolution_convert_fusion.1
  13.7 0.0 copy-done
  13.7 2.2 convolution_convert_fusion.2
  15.9 252.6 %rows_to_experts.1 = (bf16[2,4,72,7168]{3,2,1,0:T(8,128)(2,1)}, bf16[2,4,72,7168]{3,2,1,0:T(8,128)(2,1)}, bf16[2,4,72,7168]{3,2,1,0:T(8,128)(2,1)}, bf16[1,128,7...) custom-call(bf16[2,72,7168]{2,1,0:T(8,128)(2,1)} %bitcast.102, ...), custom_call_target="tpu_custom_call" | custom-call | tf_op jit(solution)/shard_map/rows_to_experts/pallas_call | solution.py:224
  268.6 0.9 slice_reduce_fusion
  269.5 0.0 copy-start.2
  269.5 0.0 copy-start.4
  269.5 0.0 slice-start
  269.5 6.9 %fusion.14 = f32[576,256]{1,0:T(8,128)S(1)} fusion(bf16[576,7168]{1,0:T(8,128)(2,1)} %bitcast.115, bf16[1,256,7168]{2,1,0:T(8,128)(2,1)} %param.21), kind=kOutput, calls=%fused_computation.29 | convolution fusion | flops 2113929216 | bytes 12517376 | tf_op jit(solution)/shard_map/dot_general | solution.py:53
  276.4 0.0 copy-done.2
  276.4 0.9 copy-done.4
  277.3 0.0 slice-start.1
  277.3 2.3 fusion.24
  279.6 0.0 slice-done
  279.6 0.3 slice-done.1
  279.9 2.3 fusion.26
  282.2 17.6 %convolution_convert_fusion = bf16[576,7168]{1,0:T(8,128)(2,1)} fusion(bf16[1,256,7168]{2,1,0:T(8,128)(2,1)} %param.21, bf16[576,7168]{1,0:T(8,128)(2,1)} %bitcast.96, bf16[1,7168,256]{2,1,0:T(8,128)(2,1)} %param.20, f32[576,256]{1,0:T(8,128)S(1)} %fusion.26), kind=kOutput, calls=%fused_computation.1 | convolution fusion | flops 4232871936 | bytes 24444928 | tf_op jit(solution)/shard_map/dot_general | solution.py:46
  299.8 19.8 %fusion.22 = f32[576,7168]{1,0:T(8,128)} fusion(bf16[1,7168,256]{2,1,0:T(8,128)(2,1)} %param.19, f32[576,256]{1,0:T(8,128)S(1)} %fusion.14, bf16[576,7168]{1,0:T(8,128)(2,1)} %bitcast.94, bf16[1,7168,256]{2,1,0:T(8,128)(2,1)} %param.20, f32[576,256]{1,0:T(8,128)S(1)} %fusion.24), kind=kOutput, calls=%fused_computation.37 | convolution fusion | flops 4229332992 | bytes 33292288 | tf_op jit(solution)/shard_map/dot_general | solution.py:59
  319.6 12.6 %add_convert_fusion = bf16[576,7168]{1,0:T(8,128)(2,1)} fusion(f32[576,7168]{1,0:T(8,128)} %fusion.22, bf16[1,7168,256]{2,1,0:T(8,128)(2,1)} %param.20, f32[576,256]{1,0:T(8,128)S(1)} %fusion.14, f32[576,256]{1,0:T(8,128)S(1)} %fusion.24), kind=kOutput, calls=%fused_computation | convolution fusion | flops 2123071488 | bytes 29622272 | tf_op jit(solution)/shard_map/dot_general | solution.py:60
  332.2 0.0 copy-start.7
  332.2 177.3 %sums_to_tokens.1 = (bf16[2,72,7168]{2,1,0:T(8,128)(2,1)}, bf16[2,72,7168]{2,1,0:T(8,128)(2,1)}) custom-call(bf16[2,4,72,7168]{3,2,1,0:T(8,128)(2,1)} %bitcast.93, bf16[2,4,72,7168]{3,2,1,0:T(8,128)(2,1)} %bitcast.92), custom_call_target="tpu_custom_call" | custom-call | tf_op jit(solution)/shard_map/sums_to_tokens/pallas_call | solution.py:394
  509.5 0.0 copy-start.3
  509.5 0.0 copy-start.5
  509.5 0.0 copy-start.9
  509.5 0.0 copy-start.11
  509.6 0.0 copy-done.7
  509.6 0.0 copy-done.10
  509.6 3.6 fusion.3
  513.2 0.0 copy-done.3
  513.2 0.0 copy-done.5
  513.2 0.0 copy-done.9
  513.2 0.0 copy-done.11
  513.2 0.0 copy-start.6
  513.3 1.3 fusion.12
  514.6 0.2 copy-done.6
  514.7 2.3 fusion.28
  (7 shorter events, 0.0 us)
Async XLA Ops:
  0.6 6.0 %copy-start.13 = (s32[1,128,1]{1,2,0:T(1,128)S(1)}, s32[1,128,1]{1,2,0:T(1,128)}, u32[]{:S(2)}) copy-start(s32[1,128,1]{1,2,0:T(1,128)} %param.16) | copy-start | bytes 1540
  0.6 4.8 copy-start.12
  0.7 6.4 %copy-start.15 = (f32[1,128,1]{1,2,0:T(1,128)S(1)}, f32[1,128,1]{1,2,0:T(1,128)}, u32[]{:S(2)}) copy-start(f32[1,128,1]{1,2,0:T(1,128)} %param.17) | copy-start | bytes 1540
  0.7 4.1 copy-start.14
  2.6 9.1 %copy-start.1 = (bf16[1,128,7168]{2,1,0:T(8,128)(2,1)S(1)}, bf16[1,128,7168]{2,1,0:T(8,128)(2,1)}, u32[]{:S(2)}) copy-start(bf16[1,128,7168]{2,1,0:T(8,128)(2,1)} %refs_6_.1) | copy-start | bytes 5505028
  2.6 9.0 %copy-start.8 = (f32[1,7168]{1,0:T(1,128)S(1)}, f32[1,7168]{1,0:T(1,128)}, u32[]{:S(2)}) copy-start(f32[1,7168]{1,0:T(1,128)} %param.18) | copy-start | bytes 86020
  8.0 5.8 %copy-start = (bf16[1,128,7168]{2,1,0:T(8,128)(2,1)S(1)}, bf16[1,128,7168]{2,1,0:T(8,128)(2,1)}, u32[]{:S(2)}) copy-start(bf16[1,128,7168]{2,1,0:T(8,128)(2,1)} %refs_3_.1) | copy-start | bytes 5505028
  269.5 6.9 %copy-start.2 = (bf16[2,4,72,7168]{3,2,1,0:T(8,128)(2,1)S(1)}, bf16[2,4,72,7168]{3,2,1,0:T(8,128)(2,1)}, u32[]{:S(2)}) copy-start(bf16[2,4,72,7168]{3,2,1,0:T(8,128)(2,1)} %get-tuple-element.19) | copy-start | bytes 24772612
  269.5 7.8 %copy-start.4 = (bf16[1,7168,256]{2,1,0:T(8,128)(2,1)S(1)}, bf16[1,7168,256]{2,1,0:T(8,128)(2,1)}, u32[]{:S(2)}) copy-start(bf16[1,7168,256]{2,1,0:T(8,128)(2,1)} %param.19) | copy-start | bytes 11010052
  269.5 10.1 %slice-start = ((s8[8257536]{0:T(1024)(128)(4,1)}), s8[4194304]{0:T(1024)(128)(4,1)S(1)}, s32[]{:S(2)}) async-start(s8[8257536]{0:T(1024)(128)(4,1)} %bitcast.97), calls=%async_computation | async-start | bytes 8388608
  277.3 2.6 slice-start.1
  332.2 177.4 %copy-start.7 = (bf16[1,128,7168]{2,1,0:T(8,128)(2,1)S(1)}, bf16[1,128,7168]{2,1,0:T(8,128)(2,1)}, u32[]{:S(2)}) copy-start(bf16[1,128,7168]{2,1,0:T(8,128)(2,1)} %get-tuple-element.14) | copy-start | bytes 5505028
  332.2 177.4 %copy-start.10 = (bf16[128,256]{1,0:T(8,128)(2,1)S(1)}, bf16[128,256]{1,0:T(8,128)(2,1)}, u32[]{:S(2)}) copy-start(bf16[128,256]{1,0:T(8,128)(2,1)} %get-tuple-element.16) | copy-start | bytes 196612
  509.5 3.7 copy-start.3
  509.5 3.7 copy-start.5
  509.5 3.7 copy-start.9
  509.5 3.7 copy-start.11
  513.2 1.5 copy-start.6

commit v5 on v4

--- a/solution.py
+++ b/solution.py
@@ -39,11 +39,10 @@
     return jnp.dot(select, rows, preferred_element_type=jnp.float32)
 
 
-def expert_forward(token_rows, gate_cols, up_cols, down_rows):
+def expert_forward(token_rows, gate_cols, up_cols):
     pre_gate = jnp.dot(token_rows, gate_cols, preferred_element_type=jnp.float32)
     pre_up = jnp.dot(token_rows, up_cols, preferred_element_type=jnp.float32)
-    hidden = (pre_gate * jax.nn.sigmoid(pre_gate) * pre_up).astype(jnp.bfloat16)
-    return jnp.dot(hidden, down_rows, preferred_element_type=jnp.float32)
+    return (pre_gate * jax.nn.sigmoid(pre_gate) * pre_up).astype(jnp.bfloat16)
 
 
 def expert_backward(token_rows, upstream, gate_cols, up_cols, down_rows):
@@ -56,9 +55,7 @@
         grad_hidden * pre_up * sigmoid_gate * (1.0 + pre_gate * (1.0 - sigmoid_gate))
     ).astype(jnp.bfloat16)
     grad_up = (grad_hidden * pre_gate * sigmoid_gate).astype(jnp.bfloat16)
-    first = lax.dot_general(grad_gate, gate_cols, contract, preferred_element_type=jnp.float32)
-    second = lax.dot_general(grad_up, up_cols, contract, preferred_element_type=jnp.float32)
-    return first + second
+    return grad_gate, grad_up
 
 
 MESH = pl.DeviceIdType.MESH
@@ -259,8 +256,10 @@
 
 def return_kernel(experts_n, shifts, *refs):
     arrays = len(shifts)
-    partial, summed = refs[:arrays], refs[arrays : 2 * arrays]
+    hidden, grad_gate, grad_up, gate_cols, up_cols, down_rows = refs[:6]
+    summed = refs[6 : 6 + arrays]
     (
+        all_partial,
         far_first,
         far_second,
         near_in,
@@ -271,7 +270,8 @@
         near_recv,
         out_send,
         out_recv,
-    ) = refs[2 * arrays :]
+    ) = refs[6 + arrays :]
+    partial = [all_partial.at[a] for a in range(arrays)]
     far_in = (far_first, far_second)
     group, shard, links, far = places(experts_n)
     here = section_at(0)
@@ -283,7 +283,34 @@
             for expert in range(experts_n)
         ]
     )
-    width = partial[0].shape[3] // CHUNKS
+    capacity, features = summed[0].shape[1:]
+    width = features // CHUNKS
+    contract = (((1,), (1,)), ((), ()))
+
+    def product(a, block, at):
+        rows = (hidden,) if a == 0 else (grad_gate, grad_up)
+        rows = [ref[...] if block is None else ref[block] for ref in rows]
+        if a == 0:
+            return jnp.dot(rows[0], down_rows[:, at], preferred_element_type=jnp.float32)
+        return lax.dot_general(
+            rows[0], gate_cols[at, :], contract, preferred_element_type=jnp.float32
+        ) + lax.dot_general(rows[1], up_cols[at, :], contract, preferred_element_type=jnp.float32)
+
+    def compute(a, c):
+        tile = 512 if width % 512 == 0 else 128
+
+        @pl.loop(0, width // tile)
+        def _(i):
+            at = pl.ds(pl.multiple_of(c * width + i * tile, tile), tile)
+            if len(hidden.shape) == 2:
+                block = product(a, None, at).reshape(experts_n, SHARDS, capacity, tile)
+                all_partial[a, :, :, :, at] = block.astype(jnp.bfloat16)
+            else:
+                for o in range(experts_n):
+                    for d in range(SHARDS):
+                        block = product(a, o * SHARDS + d, at)
+                        all_partial[a, o, d, :, at] = block.astype(jnp.bfloat16)
+
     started, far_copies, near_copies, out_copies = [], {}, {}, {}
 
     def begin(copy):
@@ -301,7 +328,12 @@
     def columns(c):
         return pieces(width, experts_n, c * width)
 
+    computed = set()
+
     def send(a, step, c):
+        if (a, c) not in computed:
+            computed.add((a, c))
+            compute(a, c)
         origin = (group + step) % experts_n
         cols = columns(c)
         for side, target in enumerate(links):
@@ -385,18 +417,22 @@
         copy.wait_send()
 
 
-def return_call(partial, shifts):
-    arrays = len(partial)
-    experts_n, unused, capacity, features = partial[0].shape
+def return_call(rows, weights, experts_n, shifts):
+    arrays = len(shifts)
+    features = weights[0].shape[0]
+    capacity = rows[0].shape[0] // (experts_n * SHARDS)
+    if capacity % 8 != 0:
+        rows = [value.reshape(experts_n * SHARDS, capacity, -1) for value in rows]
     dma = pltpu.SemaphoreType.DMA
     shape = jax.ShapeDtypeStruct((experts_n, capacity, features), jnp.bfloat16)
     first, second = pieces(features // CHUNKS, experts_n)
     return pl.pallas_call(
         functools.partial(return_kernel, experts_n, shifts),
         out_shape=[shape] * arrays,
-        in_specs=[pl.BlockSpec(memory_space=pltpu.VMEM)] * arrays,
+        in_specs=[pl.BlockSpec(memory_space=pltpu.VMEM)] * 6,
         out_specs=[pl.BlockSpec(memory_space=pl.ANY)] * arrays,
         scratch_shapes=[
+            pltpu.VMEM((arrays, experts_n, SHARDS, capacity, features), jnp.bfloat16),
             pltpu.VMEM((arrays, experts_n, CHUNKS, capacity, first.size), jnp.bfloat16),
             pltpu.VMEM((arrays, experts_n, CHUNKS, capacity, second.size), jnp.bfloat16),
             pltpu.VMEM((arrays, experts_n, 2, capacity, features), jnp.bfloat16),
@@ -412,7 +448,7 @@
             collective_id=1, has_side_effects=True, vmem_limit_bytes=VMEM_BYTES
         ),
         name="sums_to_tokens",
-    )(*partial)
+    )(*rows, *weights)
 
 
 def local(
@@ -465,15 +501,12 @@
         packed, [value for value, by in passed], tuple(by for value, by in passed)
     )
     all_fwd, all_bwd, all_grad = [rows.reshape(-1, features) for rows in gathered]
-    results = (
-        expert_forward(all_fwd, gate_cols, up_cols, down_rows),
-        expert_backward(all_bwd, all_grad, gate_cols, up_cols, down_rows),
-    )
-    partial = [
-        result.astype(jnp.bfloat16).reshape(experts_n, SHARDS, capacity, features)
-        for result in results
-    ]
-    back_fwd, back_bwd = [rows.reshape(-1, features) for rows in return_call(partial, (1, -1))]
+    hidden = expert_forward(all_fwd, gate_cols, up_cols)
+    grad_gate, grad_up = expert_backward(all_bwd, all_grad, gate_cols, up_cols, down_rows)
+    sums = return_call(
+        (hidden, grad_gate, grad_up), (gate_cols, up_cols, down_rows), experts_n, (1, -1)
+    )
+    back_fwd, back_bwd = [rows.reshape(-1, features) for rows in sums]
     acts, table_fwd, gates, stash, grads, table_bwd, gain_there = arrived
     filled = experts_n * capacity
     mixture = gates[:, :1] * pick(table_fwd[:, :filled], back_fwd)

time: 519 us -> 478 us (0.921)
  matrix products: 74.4 us -> 34 us
    dot_general x3 -> x2, matrix products: 50 us -> 6.35 us  [the longest x1 3.21 us: expert_forward(): pre_up = jnp.dot(token_rows, up_cols, preferred_element_type=jnp.float32)]
where the time goes in v5:
time: 478 us; the launch traced here: 477 us
  Pallas kernels  431 us (90%)
  matrix products  34 us (7%)
  other arithmetic  7.48 us (2%)
    pallas_call x1, Pallas kernels, outward_call(): pl.pallas_call(functools.partial(outward_kernel, experts_n, arrays, shift...  253 us
    pallas_call x1, Pallas kernels, return_call(): pl.pallas_call(functools.partial(return_kernel, experts_n, shifts), out_s...  178 us
    dot_general x5, matrix products, pick(): return jnp.dot(select, rows, preferred_element_type=jnp.float32)  12.9 us

profile of v5, /device:TPU:0, one launch (start us, length us, event | category | flops | bytes accessed | tf_op | source)
XLA Modules:
  0.0 476.5 jit_solution(11594726865810032224)
XLA Ops:
  0.6 0.0 copy-start.14
  0.6 0.0 copy-start.13
  0.7 0.0 copy-start.16
  0.7 0.0 copy-start.15
  0.7 1.9 fusion.4
  2.6 0.0 copy-start.1
  2.6 0.0 copy-start.9
  2.6 2.1 fusion.7
  4.7 0.0 copy-done.15
  4.7 0.7 broadcast_in_dim.44.refs_5_
  5.4 0.0 copy-done.13
  5.5 0.1 fusion.31
  5.5 0.2 reduce_window_sum.17
  5.7 0.2 select_reduce_fusion.2
  5.9 0.1 convert_convert_fusion.1
  6.0 0.6 pad.7.refs_4_
  6.6 0.0 copy-done.14
  6.6 0.1 fusion.30
  6.7 0.2 reduce_window_sum.18
  6.9 0.2 select_reduce_fusion.1
  7.1 0.0 copy-done.16
  7.1 0.1 select_reduce_fusion
  7.2 0.1 convert_convert_fusion
  7.3 0.6 pad.8.refs_8_
  8.0 3.7 fusion.1
  11.7 0.0 copy-done.1
  11.7 0.0 copy-done.9
  11.7 2.1 convolution_convert_fusion
  13.8 0.0 copy-done
  13.8 2.2 convolution_convert_fusion.1
  16.0 252.6 %rows_to_experts.1 = (bf16[2,4,72,7168]{3,2,1,0:T(8,128)(2,1)}, bf16[2,4,72,7168]{3,2,1,0:T(8,128)(2,1)}, bf16[2,4,72,7168]{3,2,1,0:T(8,128)(2,1)}, bf16[1,128,7...) custom-call(bf16[2,72,7168]{2,1,0:T(8,128)(2,1)} %bitcast.72, ...), custom_call_target="tpu_custom_call" | custom-call | tf_op jit(solution)/shard_map/rows_to_experts/pallas_call | solution.py:221
  268.6 0.9 slice_reduce_fusion
  269.5 0.0 copy-done.3
  269.5 0.0 copy-start.5
  269.6 0.0 slice-start.2
  269.6 5.8 %fusion.45 = f32[576,256]{1,0:T(8,128)S(1)} fusion(bf16[576,7168]{1,0:T(8,128)(2,1)} %bitcast.92, bf16[1,7168,256]{2,1,0:T(8,128)(2,1)S(1)} %copy-done.3), kind=kOutput, calls=%fused_computation.78 | convolution fusion | flops 2113929216 | bytes 12517376 | tf_op jit(solution)/shard_map/dot_general | solution.py:49
  275.4 0.0 copy-done.5
  275.4 0.0 copy-start.4
  275.4 0.0 slice-start.3
  275.4 0.0 slice-start
  275.4 6.5 %multiply_convert_fusion = (bf16[576,256]{1,0:T(8,128)(2,1)}, f32[576,256]{1,0:T(8,128)S(1)}) fusion(f32[576,256]{1,0:T(8,128)S(1)} %fusion.45, bf16[576,7168]{1,0:T(8,128)(2,1)} %bitcast.96, bf16[1,256,7168]{2,1,0:T(8,128)(2,1)S(1)} %copy-done.5), kind=kOutput, calls=%fused_computation.41 | convolution fusion | flops 2114813952 | bytes 13402112 | tf_op jit(solution)/shard_map/dot_general | solution.py:52
  282.0 0.0 slice-done.2
  282.0 0.0 copy-done.4
  282.0 0.0 slice-done.3
  282.0 0.0 slice-start.1
  282.0 3.1 fusion.26.refs_1_
  285.1 0.0 slice-done
  285.1 0.0 slice-done.1
  285.1 2.4 fusion.47
  287.5 3.2 fusion.27.refs_0_
  290.7 178.3 %sums_to_tokens.1 = (bf16[2,72,7168]{2,1,0:T(8,128)(2,1)}, bf16[2,72,7168]{2,1,0:T(8,128)(2,1)}) custom-call(bf16[576,256]{1,0:T(8,128)(2,1)} %fusion.27.refs_0_, bf16[576,256]{1,0:T(8,128)(2,1)} %fusion.26.refs_1_, bf16[576,256]{1,0:T(8,128)(2,1)} %get-tuple-element.30.refs_2_, bf16[7168,256]{1,0:T(8,128)(2,1)} %bitcast.73, bf16[7168,256]{1,0:T(8,128)(2,1)} %bitcast.74, ...), custom_call_target="tpu_custom_call" | custom-call | tf_op jit(solution)/shard_map/sums_to_tokens/pallas_call | solution.py:429
  469.0 0.0 copy-start.2
  469.0 0.0 copy-start.6
  469.0 0.0 copy-start.10
  469.0 0.0 copy-start.12
  469.0 0.0 copy-done.8
  469.0 0.0 copy-done.11
  469.0 3.6 fusion.3
  472.7 0.0 copy-done.2
  472.7 0.0 copy-done.12
  472.7 0.0 copy-start.7
  472.7 1.3 fusion.12
  474.0 0.2 copy-done.7
  474.2 2.3 fusion.14
  (13 shorter events, 0.0 us)
Async XLA Ops:
  0.6 6.0 %copy-start.14 = (s32[1,128,1]{1,2,0:T(1,128)S(1)}, s32[1,128,1]{1,2,0:T(1,128)}, u32[]{:S(2)}) copy-start(s32[1,128,1]{1,2,0:T(1,128)} %param.16) | copy-start | bytes 1540
  0.6 4.8 %copy-start.13 = (s32[1,128,1]{1,2,0:T(1,128)S(1)}, s32[1,128,1]{1,2,0:T(1,128)}, u32[]{:S(2)}) copy-start(s32[1,128,1]{1,2,0:T(1,128)} %param.12) | copy-start | bytes 1540
  0.7 6.4 %copy-start.16 = (f32[1,128,1]{1,2,0:T(1,128)S(1)}, f32[1,128,1]{1,2,0:T(1,128)}, u32[]{:S(2)}) copy-start(f32[1,128,1]{1,2,0:T(1,128)} %param.17) | copy-start | bytes 1540
  0.7 4.1 copy-start.15
  2.6 9.1 %copy-start.1 = (bf16[1,128,7168]{2,1,0:T(8,128)(2,1)S(1)}, bf16[1,128,7168]{2,1,0:T(8,128)(2,1)}, u32[]{:S(2)}) copy-start(bf16[1,128,7168]{2,1,0:T(8,128)(2,1)} %refs_6_.1) | copy-start | bytes 5505028
  2.6 9.0 %copy-start.9 = (f32[1,7168]{1,0:T(1,128)S(1)}, f32[1,7168]{1,0:T(1,128)}, u32[]{:S(2)}) copy-start(f32[1,7168]{1,0:T(1,128)} %param.18) | copy-start | bytes 86020
  8.0 5.8 %copy-start = (bf16[1,128,7168]{2,1,0:T(8,128)(2,1)S(1)}, bf16[1,128,7168]{2,1,0:T(8,128)(2,1)}, u32[]{:S(2)}) copy-start(bf16[1,128,7168]{2,1,0:T(8,128)(2,1)} %refs_3_.1) | copy-start | bytes 5505028
  16.0 253.6 %copy-start.3 = (bf16[1,7168,256]{2,1,0:T(8,128)(2,1)S(1)}, bf16[1,7168,256]{2,1,0:T(8,128)(2,1)}, u32[]{:S(2)}) copy-start(bf16[1,7168,256]{2,1,0:T(8,128)(2,1)} %param.19) | copy-start | bytes 11010052
  269.5 5.8 %copy-start.5 = (bf16[1,256,7168]{2,1,0:T(8,128)(2,1)S(1)}, bf16[1,256,7168]{2,1,0:T(8,128)(2,1)}, u32[]{:S(2)}) copy-start(bf16[1,256,7168]{2,1,0:T(8,128)(2,1)} %param.21) | copy-start | bytes 11010052
  269.6 12.4 %slice-start.2 = ((s8[8257536]{0:T(1024)(128)(4,1)}), s8[4194304]{0:T(1024)(128)(4,1)S(1)}, s32[]{:S(2)}) async-start(s8[8257536]{0:T(1024)(128)(4,1)} %bitcast.93), calls=%async_computation.2 | async-start | bytes 8388608
  275.4 6.6 %copy-start.4 = (bf16[1,7168,256]{2,1,0:T(8,128)(2,1)S(1)}, bf16[1,7168,256]{2,1,0:T(8,128)(2,1)}, u32[]{:S(2)}) copy-start(bf16[1,7168,256]{2,1,0:T(8,128)(2,1)} %param.20) | copy-start | bytes 11010052
  275.4 6.6 %slice-start.3 = ((s8[8257536]{0:T(1024)(128)(4,1)}), s8[4063232]{0:T(1024)(128)(4,1)S(1)}, s32[]{:S(2)}) async-start(s8[8257536]{0:T(1024)(128)(4,1)} %bitcast.93), calls=%async_computation.3 | async-start | bytes 8126464
  275.4 9.7 %slice-start = ((s8[8257536]{0:T(1024)(128)(4,1)}), s8[4063232]{0:T(1024)(128)(4,1)S(1)}, s32[]{:S(2)}) async-start(s8[8257536]{0:T(1024)(128)(4,1)} %bitcast.88), calls=%async_computation | async-start | bytes 8126464
  282.0 3.2 slice-start.1
  290.7 178.3 %copy-start.8 = (bf16[1,128,7168]{2,1,0:T(8,128)(2,1)S(1)}, bf16[1,128,7168]{2,1,0:T(8,128)(2,1)}, u32[]{:S(2)}) copy-start(bf16[1,128,7168]{2,1,0:T(8,128)(2,1)} %get-tuple-element.14) | copy-start | bytes 5505028
  290.7 178.3 %copy-start.11 = (bf16[128,256]{1,0:T(8,128)(2,1)S(1)}, bf16[128,256]{1,0:T(8,128)(2,1)}, u32[]{:S(2)}) copy-start(bf16[128,256]{1,0:T(8,128)(2,1)} %get-tuple-element.16) | copy-start | bytes 196612
  469.0 3.7 copy-start.2
  469.0 3.7 copy-start.6
  469.0 3.7 copy-start.10
  469.0 3.7 copy-start.12
  472.7 1.5 copy-start.7
